TPU v7x, 256 devices: a whole 4x4x8 slice. The times are simulated.
256 devices in a mesh: row: 32 (over z, x_lo, core), rep: 8 (over x_hi, y).
Axes of the slice: x: 4 (x_hi: 2, x_lo: 2; x = x_hi * 2 + x_lo), y: 4, z: 8, core: 2. Of those that a mesh axis runs over, the one named last changes fastest.
Arguments:
- features: bfloat16 [65536, 128], P(('row', 'rep')), may hold values from -6 to 6
- tile_values: bfloat16 [65536, 128, 128], P(('row', 'rep')), may hold values from 0 to 100, as said below
- tile_rows: int32 [256, 256], P(('row', 'rep')), may hold values from 0 to 15
- tile_cols: int32 [256, 256], P(('row', 'rep')), may hold values from 0 to 1
- tile_count: int32 [256, 32], P(('row', 'rep')), may hold values from 1 to 8, as said below
- weight: bfloat16 [128, 256], replicated, may hold values from -6 to 6
- bias: float32 [256], replicated, may hold values from -3 to 3
- cotangent: bfloat16 [65536, 256], P(('row', 'rep')), may hold values from -6 to 6
Outputs:
- hidden_out: bfloat16 [65536, 256], P(('row', 'rep'))
- grad_features: bfloat16 [65536, 128], P(('row', 'rep'))
- grad_weight: float32 [128, 256], replicated
Inputs may be any that keep to these rules, and one draw needn't show every extreme that they name: `tile_values`: nonnegative edge weights, zero where a tile has no edge. `tile_count`: in every device some source block has all 8 slots live.
All inputs are finite; a program needn't handle non-finite values.
Results may differ from a plain program's by a relative error of at most 0.012.
Values may be sent and summed in bfloat16 or wider, within the bound.
No kernel may reach another device: no remote copies, remote signals or barrier semaphores. Data moves between devices by JAX's collectives and lax.ppermute only.
A program may use at most 128 MiB of HBM per device.

v0:
```python
import jax
import jax.numpy as jnp
from jax import lax
from jax.sharding import PartitionSpec as P


def activate(pre_values, upstream):
    output, pullback = jax.vjp(lambda v: jax.nn.gelu(v, approximate=True), pre_values)
    (slope,) = pullback(upstream.astype(pre_values.dtype))
    return (output, slope)


def body(features, tile_values, tile_rows, tile_cols, tile_count, weight, bias, cotangent):
    cycle_size = lax.axis_size("row")
    replicas = lax.axis_size("rep")
    sub_rows = features.shape[0]
    tile_size = tile_values.shape[1]
    feature_width = features.shape[1]
    block_rows = sub_rows * replicas
    row_tiles = block_rows // tile_size
    col_tiles = sub_rows // tile_size
    slot_total = tile_values.shape[0]
    slot_width = slot_total // cycle_size
    replica_index = lax.axis_index("rep")
    own_offset = replica_index * sub_rows
    slot_order = lax.broadcasted_iota(jnp.int32, (cycle_size, slot_width), 1)
    live = (slot_order < tile_count[0][:, None]).astype(jnp.float32).reshape(slot_total)
    tile_index = lax.broadcasted_iota(jnp.int32, (slot_total, row_tiles), 1)
    row_hot = (tile_rows[0][:, None] == tile_index).astype(jnp.float32) * live[:, None]
    slot_columns = tile_cols[0]
    row_weights = jnp.sum(tile_values, axis=2, dtype=jnp.float32)
    partial_degree = jnp.einsum(
        "sr,sk->rk", row_hot, row_weights, precision=lax.Precision.HIGHEST
    ).reshape(block_rows)
    degree = 1.0 + lax.psum(partial_degree, "rep")
    scale_all = lax.rsqrt(degree)
    scale_own = lax.dynamic_slice_in_dim(scale_all, own_offset, sub_rows)
    scaled = (scale_own[:, None] * features.astype(jnp.float32)).astype(jnp.bfloat16)
    segment = lax.all_gather(scaled, "row", axis=0, tiled=True)
    length = segment.shape[0]
    block_span = min(cycle_size, -(-length // sub_rows))
    lead_block = jnp.clip(jnp.int32(0) // sub_rows, 0, cycle_size - block_span)
    span_slots = block_span * slot_width
    part_tiles = tile_values
    part_columns = slot_columns
    part_hot = row_hot
    block_of = lead_block + lax.broadcasted_iota(jnp.int32, (span_slots,), 0) // slot_width
    anchor = block_of * sub_rows + part_columns * tile_size
    positions = anchor[:, None] + lax.broadcasted_iota(jnp.int32, (span_slots, tile_size), 1)
    inside = (positions >= 0) & (positions < length)
    picked = jnp.take(segment, jnp.clip(positions, 0, length - 1).reshape(-1), axis=0)
    picked = picked.reshape(span_slots, tile_size, feature_width)
    picked = jnp.where(inside[:, :, None], picked, jnp.zeros_like(picked))
    products = jnp.einsum("skt,stf->skf", part_tiles, picked, preferred_element_type=jnp.float32)
    neighbours = jnp.einsum(
        "sr,skf->rkf", part_hot, products, precision=lax.Precision.HIGHEST
    ).reshape(block_rows, feature_width)
    own_part = lax.dynamic_slice_in_dim(neighbours, own_offset, sub_rows, 0) + scaled.astype(
        jnp.float32
    )
    partial_value = lax.dynamic_update_slice_in_dim(neighbours, own_part, own_offset, 0)
    total = lax.psum(partial_value, "rep")
    agg_b = (scale_all[:, None] * total).astype(jnp.bfloat16)
    pre = jnp.dot(agg_b, weight, preferred_element_type=jnp.float32) + bias
    full_cotangent = lax.all_gather(cotangent, "rep", axis=0, tiled=True)
    output, slope = activate(pre, full_cotangent)
    dpre = slope.astype(jnp.bfloat16)
    hidden_out = lax.dynamic_slice_in_dim(output, own_offset, sub_rows, 0).astype(jnp.bfloat16)
    weight_term = lax.dot_general(
        agg_b, dpre, (((0,), (0,)), ((), ())), preferred_element_type=jnp.float32
    )
    grad_weight = lax.psum(weight_term, "row")
    back_full = jnp.einsum("nh,fh->nf", dpre, weight, preferred_element_type=jnp.float32)
    back_all = (scale_all[:, None] * back_full).astype(jnp.bfloat16)
    back_own = lax.dynamic_slice_in_dim(back_all, own_offset, sub_rows, 0)
    back_tiles = back_all.reshape(row_tiles, tile_size, feature_width)
    hot_narrow = row_hot.astype(jnp.bfloat16)
    block_span = lax.axis_size("row") * sub_rows // sub_rows
    part_tiles = tile_values
    part_columns = slot_columns
    part_hot = hot_narrow
    chosen = jnp.einsum(
        "sr,rkf->skf", part_hot, back_tiles, preferred_element_type=jnp.float32
    ).astype(jnp.bfloat16)
    products = jnp.einsum("skt,skf->stf", part_tiles, chosen, preferred_element_type=jnp.float32)
    products = products.reshape(block_span, slot_width, tile_size, feature_width)
    block_columns = part_columns.reshape(block_span, slot_width)
    column_index = lax.broadcasted_iota(jnp.int32, (block_span, slot_width, col_tiles), 2)
    target_hot = (block_columns[:, :, None] == column_index).astype(jnp.float32)
    placed = jnp.einsum("bsc,bstf->bctf", target_hot, products, precision=lax.Precision.HIGHEST)
    incoming = lax.psum_scatter(
        placed.reshape(lax.axis_size("row") * sub_rows, feature_width),
        "row",
        scatter_dimension=0,
        tiled=True,
    )
    grad_features = (scale_own[:, None] * (incoming + back_own.astype(jnp.float32))).astype(
        jnp.bfloat16
    )
    return (hidden_out, grad_features, grad_weight)


def solution(mesh):
    placed = (
        P(("row", "rep"), None),
        P(("row", "rep"), None, None),
        P(("row", "rep"), None),
        P(("row", "rep"), None),
        P(("row", "rep"), None),
        P(),
        P(),
        P(("row", "rep"), None),
    )
    return jax.shard_map(
        body,
        mesh=mesh,
        in_specs=placed,
        out_specs=(P(("row", "rep"), None), P(("row", "rep"), None), P()),
        check_vma=False,
    )
```

profile of v0, /device:TPU:2, one launch (start us, length us, event | category | flops | bytes accessed | tf_op | source)
XLA Modules:
  0.0 757.1 jit_solution(452279704625792501)
XLA Ops:
  7.2 0.0 copy-start
  7.2 0.0 all-gather.3.cloned.1.call-start
  7.2 0.7 fusion.35
  8.0 0.1 reshape.142
  8.0 0.0 copy-start.5
  8.1 0.0 copy-start.4
  8.1 0.0 copy-start.6
  8.1 5.7 convert_reduce_fusion
  13.8 0.0 copy-done.5
  13.8 0.2 convolution_bitcast_fusion
  14.0 23.8 %psum.21 = f32[2048]{0:T(1024)S(1)} all-reduce(f32[2048]{0:T(1024)S(1)} %convolution_bitcast_fusion), channel_id=1, replica_groups=mesh['row'=32,'rep'=8] {'rep'}, use_global_device_ids=true, to_apply=%region_1.0 | all-reduce | flops 2048 | bytes 16384 | tf_op jit(solution)/shard_map/psum | solution.py:35
  37.8 0.1 dynamic_slice.12
  37.8 0.0 copy-done.4
  37.8 0.7 multiply_convert_fusion.2
  38.6 0.0 all-gather.3.cloned.1.call-update
  38.6 0.0 all-gather.5.cloned.1.call-start
  38.7 0.7 all-gather.5.cloned.1.call-update
  39.4 0.0 all-reduce.3.cloned.1.call-start
  39.4 0.5 broadcast.184
  39.9 0.0 copy-done.6
  39.9 0.7 fusion.55
  40.6 0.2 fusion.28
  40.8 0.1 fusion.25
  40.9 0.1 compare_select_fusion
  41.0 61.3 %all-gather.3.cloned.1.call-done = bf16[8192,128]{1,0:T(8,128)(2,1)} async-done(((bf16[256,128]{1,0:T(8,128)(2,1)}), bf16[8192,128]{1,0:T(8,128)(2,1)}) %all-gather.3.cloned.1.call-update) | async-done | bytes 2097168 | tf_op jit(solution)/shard_map/all_gather | solution.py:39
  102.3 111.8 %gather_fusion = bf16[32768,128]{1,0:T(8,128)(2,1)} fusion(bf16[8192,128]{1,0:T(8,128)(2,1)} %all-gather.3.cloned.1.call-done, s32[32768]{0:T(1024)S(1)} %broadcast_clamp_fusion), kind=kCustom, calls=%fused_computation | custom fusion | bytes 16908288 | tf_op jit(solution)/shard_map/jit(_take)/gather | solution.py:51
  214.1 19.4 %fusion.4 = f32[256,128,128]{2,1,0:T(8,128)} fusion(bf16[256,128,128]{2,1,0:T(8,128)(2,1)} %param.9, bf16[256,128,128]{2,1,0:T(8,128)(2,1)} %bitcast.39, pred[256,128]{1,0:T(8,128)(4,1)S(1)} %get-tuple-element.8, pred[256,128]{1,0:T(8,128)(4,1)S(1)} %get-tuple-element.7), kind=kOutput, calls=%fused_computation.6 | convolution fusion | flops 1082130432 | bytes 33619968 | tf_op jit(solution)/shard_map/skt,stf->skf/dot_general | solution.py:54
  233.6 17.5 %copy.16 = f32[256,128,128]{1,0,2:T(8,128)} copy(f32[256,128,128]{2,1,0:T(8,128)} %fusion.4) | data formatting | bytes 33554432 | tf_op jit(solution)/shard_map/skt,stf->skf/dot_general | solution.py:54
  251.1 0.0 copy-start.7
  251.1 10.8 %fusion = f32[16,128,128]{2,0,1:T(8,128)S(1)} fusion(f32[256,128,128]{1,0,2:T(8,128)} %copy.16, f32[256]{0:T(256)S(1)} %reshape.142, s32[256]{0:T(256)S(1)} %bitcast.46), kind=kOutput, calls=%fused_computation.1 | convolution fusion | flops 805314560 | bytes 17827840 | tf_op jit(solution)/shard_map/sr,skf->rkf/dot_general | solution.py:55
  261.9 0.3 copy.13
  262.3 0.1 add_dynamic-update-slice_fusion
  262.4 0.0 copy-start.2
  262.4 1.0 copy-done.2
  263.4 0.0 all-reduce.3.cloned.1.call-update
  263.4 0.2 reduce-scatter.2.cloned.1.call-start
  263.6 0.1 eq.23
  263.7 0.0 all-gather.5.cloned.1.call-done
  263.7 91.8 %all-reduce.3.cloned.1.call-done = f32[2048,128]{1,0:T(8,128)} async-done(((f32[2048,128]{1,0:T(8,128)}), f32[2048,128]{1,0:T(8,128)}) %all-reduce.3.cloned.1.call-update) | async-done | bytes 1048592 | tf_op jit(solution)/shard_map/psum | solution.py:62
  355.6 0.0 copy-done
  355.6 0.0 copy-done.7
  355.6 5.4 fusion.14
  361.0 0.4 fusion.11
  361.4 5.6 fusion.22
  367.0 12.7 %copy.18 = bf16[256,128,128]{1,2,0:T(8,128)(2,1)} copy(bf16[256,128,128]{2,0,1:T(8,128)(2,1)} %fusion.22) | data formatting | bytes 16777216 | tf_op jit(solution)/shard_map/sr,rkf->skf/dot_general | solution.py:82
  379.7 13.8 %fusion.56 = f32[256,128,128]{2,1,0:T(8,128)} fusion(bf16[256,128,128]{1,2,0:T(8,128)(2,1)} %copy.18, bf16[256,128,128]{2,1,0:T(8,128)(2,1)} %param.9), kind=kOutput, calls=%fused_computation.85 | convolution fusion | flops 1073741824 | bytes 33554432 | tf_op jit(solution)/shard_map/skt,skf->stf/dot_general | solution.py:85
  393.6 17.4 %copy.14 = f32[32,8,128,128]{3,1,2,0:T(8,128)} copy(f32[32,8,128,128]{2,3,1,0:T(8,128)} %bitcast.38) | data formatting | bytes 33554432 | tf_op jit(solution)/shard_map/reshape | solution.py:86
  411.0 11.6 %fusion.29 = f32[32,2,128,128]{3,1,2,0:T(2,128)S(1)} fusion(f32[32,8,128,128]{3,1,2,0:T(8,128)} %copy.14, s32[32,8]{1,0:T(8,128)S(1)} %eq.23), kind=kOutput, calls=%fused_computation.49 | convolution fusion | flops 100663808 | bytes 20972544 | tf_op jit(solution)/shard_map/bsc,bstf->bctf/dot_general | solution.py:90
  422.6 0.0 copy-start.1
  422.7 2.5 copy.15
  425.2 0.0 copy-start.3
  425.2 0.0 reduce-scatter.2.cloned.1.call-update
  425.2 0.0 all-reduce.5.cloned.1.call-start
  425.2 1.8 fusion.24
  427.0 0.0 copy-done.3
  427.0 1.3 fusion.54
  428.4 0.0 all-reduce.5.cloned.1.call-update
  428.4 114.7 %reduce-scatter.2.cloned.1.call-done = f32[256,128]{1,0:T(8,128)} async-done(((f32[8192,128]{1,0:T(8,128)}), f32[256,128]{1,0:T(8,128)}) %reduce-scatter.2.cloned.1.call-update) | async-done | bytes 131088 | tf_op jit(solution)/shard_map/reduce_scatter | solution.py:91
  543.1 1.6 multiply_convert_fusion.1
  544.7 204.3 %all-reduce.5.cloned.1.call-done = f32[128,256]{1,0:T(8,128)} async-done(((f32[128,256]{1,0:T(8,128)}), f32[128,256]{1,0:T(8,128)}) %all-reduce.5.cloned.1.call-update) | async-done | bytes 131088 | tf_op jit(solution)/shard_map/psum | solution.py:72
  749.0 1.6 copy.25
  750.6 0.0 copy-done.1
  (3 shorter events, 0.0 us)
Async XLA Ops:
  7.2 348.4 %copy-start = (bf16[128,256]{1,0:T(8,128)(2,1)S(1)}, bf16[128,256]{1,0:T(8,128)(2,1)}, u32[]{:S(2)}) copy-start(bf16[128,256]{1,0:T(8,128)(2,1)} %param.13) | copy-start | bytes 196612
  7.2 95.1 %all-gather.3.cloned.1.call-start = ((), (), s32[]{:S(2)}) async-start(), calls=%async_computation.1 | async-start | bytes 2162688 | tf_op jit(solution)/shard_map/all_gather | solution.py:39
  8.0 5.7 copy-start.5
  8.1 29.8 %copy-start.4 = (bf16[256,128]{1,0:T(8,128)(2,1)S(1)}, bf16[256,128]{1,0:T(8,128)(2,1)}, u32[]{:S(2)}) copy-start(bf16[256,128]{1,0:T(8,128)(2,1)} %param.8) | copy-start | bytes 196612
  8.1 31.8 %copy-start.6 = (s32[1,256]{1,0:T(1,128)S(1)}, s32[1,256]{1,0:T(1,128)}, u32[]{:S(2)}) copy-start(s32[1,256]{1,0:T(1,128)} %param.11) | copy-start | bytes 3076
  38.6 225.1 %all-gather.5.cloned.1.call-start = ((), (), s32[]{:S(2)}) async-start(), calls=%async_computation.3 | async-start | bytes 1179648 | tf_op jit(solution)/shard_map/all_gather | solution.py:65
  39.4 316.2 %all-reduce.3.cloned.1.call-start = ((), (), s32[]{:S(2)}) async-start(), calls=%async_computation.2 | async-start | bytes 2097152 | tf_op jit(solution)/shard_map/psum | solution.py:62
  251.1 104.5 %copy-start.7 = (f32[256]{0:T(256)S(1)}, f32[256]{0:T(256)}, u32[]{:S(2)}) copy-start(f32[256]{0:T(256)} %param.14) | copy-start | bytes 3076
  262.4 1.0 copy-start.2
  263.4 279.7 %reduce-scatter.2.cloned.1.call-start = ((), (), s32[]{:S(2)}) async-start(), calls=%async_computation.4 | async-start | bytes 4325376 | tf_op jit(solution)/shard_map/reduce_scatter | solution.py:91
  422.6 328.0 %copy-start.1 = (bf16[128,256]{1,0:T(8,128)(2,1)S(1)}, bf16[128,256]{1,0:T(8,128)(2,1)}, u32[]{:S(2)}) copy-start(bf16[128,256]{1,0:T(8,128)(2,1)} %param.13) | copy-start | bytes 196612
  425.2 1.9 copy-start.3
  425.2 323.9 %all-reduce.5.cloned.1.call-start = ((), (), s32[]{:S(2)}) async-start(), calls=%async_computation.5 | async-start | bytes 262144 | tf_op jit(solution)/shard_map/psum | solution.py:72
Sparse Core Ops, SparseCore 0:
  38.7 63.5 all-gather.2
  105.0 50.6 all-gather.4
  263.5 92.0 all-reduce.2
  425.3 117.7 reduce-scatter.1
  546.1 202.8 all-reduce.4
where the time goes:
time: 760 us; the launch traced here: 757 us
  waiting for transfers between devices  473 us (62%)
  local copies, waits for them, and re-layouts  166 us (22%)
  matrix products  68.7 us (9%)
  blocking collectives  23.8 us (3%)
  between operations  14 us (2%)
  other arithmetic  11.8 us (2%)
    psum x1, waiting for transfers between devices, body(): grad_weight = lax.psum(weight_term, 'row')  204 us
    reduce_scatter x1, waiting for transfers between devices, body(): lax.psum_scatter(placed.reshape(lax.axis_size('row') * sub_rows, feature_...  115 us
    gather x1, local copies, waits for them, and re-layouts, body(): jnp.take(segment, jnp.clip(positions, 0, length - 1).reshape(-1), axis=0)  112 us
    psum x1, waiting for transfers between devices, body(): total = lax.psum(partial_value, 'rep')  91.8 us
    all_gather x1, waiting for transfers between devices, body(): segment = lax.all_gather(scaled, 'row', axis=0, tiled=True)  61.3 us
    psum x1, blocking collectives, body(): degree = 1.0 + lax.psum(partial_degree, 'rep')  23.8 us
    dot_general x1, matrix products, body(): jnp.einsum('skt,stf->skf', part_tiles, picked, preferred_element_type=jnp...  19.4 us
    dot_general x1, local copies, waits for them, and re-layouts, body(): jnp.einsum('skt,stf->skf', part_tiles, picked, preferred_element_type=jnp...  17.5 us
  transfers between devices with their start and end apart: 5, of which 4 were waited for; matrix products, arithmetic and copies ran while one was open for 22% of the time, Pallas kernels for 0%

commit v1 on v0

v1 whole, which is shorter than its diff:
```python
import functools

import jax
import jax.numpy as jnp
from jax import lax
from jax.experimental import pallas as pl
from jax.experimental.pallas import tpu as pltpu
from jax.sharding import Mesh, PartitionSpec as P

TILE = 128
SLOTS = 8
BF16 = jnp.bfloat16
F32 = jnp.float32
VMEM_BYTES = 48 * 1024 * 1024


def params():
    return pltpu.CompilerParams(
        dimension_semantics=("arbitrary",), vmem_limit_bytes=VMEM_BYTES
    )


def vmem():
    return pl.BlockSpec(memory_space=pltpu.VMEM)


def degree_kernel(group, row_tiles, rows, count, tiles, out, acc):
    step = pl.program_id(0)

    @pl.when(step == 0)
    def _():
        acc[...] = jnp.zeros_like(acc)

    ones = jnp.ones((16, TILE), BF16)
    for b in range(group):
        block = step * group + b
        live = count[0, block]
        stack = tiles[b * SLOTS : (b + 1) * SLOTS].reshape(SLOTS * TILE, TILE)
        sums = lax.dot_general(
            ones, stack, (((1,), (1,)), ((), ())), preferred_element_type=F32
        )
        for s in range(SLOTS):
            row = jnp.where(s < live, rows[0, block * SLOTS + s], row_tiles)
            acc[row] += sums[:8, s * TILE : (s + 1) * TILE]

    @pl.when(step == pl.num_programs(0) - 1)
    def _():
        for r in range(row_tiles):
            out[r : r + 1, :] = acc[r, 0:1, :]


def degree_call(tile_rows, tile_count, tile_values, row_tiles, group=4):
    slots = tile_values.shape[0]
    steps = slots // (SLOTS * group)
    return pl.pallas_call(
        functools.partial(degree_kernel, group, row_tiles),
        grid_spec=pltpu.PrefetchScalarGridSpec(
            num_scalar_prefetch=2,
            grid=(steps,),
            in_specs=[pl.BlockSpec((SLOTS * group, TILE, TILE), lambda i, *_: (i, 0, 0))],
            out_specs=pl.BlockSpec((row_tiles, TILE), lambda i, *_: (0, 0)),
            scratch_shapes=[pltpu.VMEM((row_tiles + 1, 8, TILE), F32)],
        ),
        out_shape=jax.ShapeDtypeStruct((row_tiles, TILE), F32),
        compiler_params=params(),
        name="degree",
    )(tile_rows, tile_count, tile_values)


def scale_kernel(copies, parts, features, row_out, col_out, spread):
    degree = 1.0 + jnp.sum(parts[...], axis=0)
    scale = lax.rsqrt(degree)
    row_out[...] = scale
    for c in range(scale.shape[0]):
        here = slice(c * TILE, (c + 1) * TILE)
        column = jnp.broadcast_to(scale[c : c + 1, :], (TILE, TILE)).T
        col_out[here, :] = column
        scaled = (column * features[here, :].astype(F32)).astype(BF16)
        for k in range(copies):
            spread[k, here, :] = scaled


def scale_call(parts, features, copies):
    sub, width = features.shape
    return pl.pallas_call(
        functools.partial(scale_kernel, copies),
        in_specs=[vmem(), vmem()],
        out_specs=(vmem(), vmem(), vmem()),
        out_shape=(
            jax.ShapeDtypeStruct((sub // TILE, TILE), F32),
            jax.ShapeDtypeStruct((sub, width), F32),
            jax.ShapeDtypeStruct((copies, sub, width), BF16),
        ),
        compiler_params=pltpu.CompilerParams(vmem_limit_bytes=VMEM_BYTES),
        name="scale",
    )(parts, features)


def forward_kernel(group, core, rows, cols, count, tiles, near, far, out, acc):
    step = pl.program_id(0)
    mine = core[0]

    @pl.when(step == 0)
    def _():
        acc[...] = jnp.zeros_like(acc)

    for b in range(group):
        for half, source in enumerate((near, far)):
            which = mine if half == 0 else 1 - mine
            first = b * 2 * SLOTS + which * SLOTS
            block = (step * group + b) * 2 + which
            live = count[0, block]
            stack = tiles[pl.ds(first, SLOTS)]
            pieces = []
            for s in range(SLOTS):
                column = cols[0, block * SLOTS + s]
                used = s < live
                tile = stack[s]
                blank = jnp.zeros_like(tile)
                left = jnp.where(used & (column == 0), tile, blank)
                right = jnp.where(used & (column != 0), tile, blank)
                pieces.append(jnp.concatenate([left, right], axis=1))
            products = jnp.dot(
                jnp.concatenate(pieces, axis=0), source[b], preferred_element_type=F32
            )
            for s in range(SLOTS):
                acc[rows[0, block * SLOTS + s]] += products[s * TILE : (s + 1) * TILE]

    @pl.when(step == pl.num_programs(0) - 1)
    def _():
        out[...] = acc[...].astype(BF16)


def forward_call(core, tile_rows, tile_cols, tile_count, tile_values, near, far, row_tiles, group=2):
    slots = tile_values.shape[0]
    steps = slots // (2 * SLOTS * group)
    sub, width = near.shape[1:]
    return pl.pallas_call(
        functools.partial(forward_kernel, group),
        grid_spec=pltpu.PrefetchScalarGridSpec(
            num_scalar_prefetch=4,
            grid=(steps,),
            in_specs=[
                pl.BlockSpec((2 * SLOTS * group, TILE, TILE), lambda i, *_: (i, 0, 0)),
                pl.BlockSpec((group, sub, width), lambda i, *_: (i, 0, 0)),
                pl.BlockSpec((group, sub, width), lambda i, *_: (i, 0, 0)),
            ],
            out_specs=pl.BlockSpec((row_tiles, TILE, width), lambda i, *_: (0, 0, 0)),
            scratch_shapes=[pltpu.VMEM((row_tiles, TILE, width), F32)],
        ),
        out_shape=jax.ShapeDtypeStruct((row_tiles, TILE, width), BF16),
        compiler_params=params(),
        name="forward",
    )(core, tile_rows, tile_cols, tile_count, tile_values, near, far)


def dense_kernel(parts, features, scale_col, scale_row, weight, bias, cotangent, hidden, back_own, pay):
    sub = features.shape[0]
    replicas = parts.shape[0]
    column = scale_col[...]
    total = (column * features[...].astype(F32)).astype(BF16).astype(F32)
    for r in range(replicas):
        total += parts[r].astype(F32)
    agg_b = (column * total).astype(BF16)
    w = weight[...]
    v = jnp.dot(agg_b, w, preferred_element_type=F32) + bias[...]
    root = 0.7978845608028654
    square = v * v
    t = jnp.tanh(root * (v + 0.044715 * (square * v)))
    cdf = 0.5 * (1.0 + t)
    hidden[...] = (v * cdf).astype(BF16)
    slope = cdf + 0.5 * v * ((1.0 - t) * (1.0 + t)) * (root * (1.0 + (3 * 0.044715) * square))
    dpre = (cotangent[...].astype(F32) * slope).astype(BF16)
    grad = lax.dot_general(agg_b, dpre, (((0,), (0,)), ((), ())), preferred_element_type=F32)
    back = lax.dot_general(w, dpre, (((1,), (1,)), ((), ())), preferred_element_type=F32)
    for c in range(sub // TILE):
        here = slice(c * TILE, (c + 1) * TILE)
        piece = (back[:, here] * scale_row[c : c + 1, :]).astype(BF16)
        back_own[here, :] = piece
        for r in range(replicas):
            pay[r, here, :] = piece
    grad_b = grad.astype(BF16)
    rows = grad.shape[0] // replicas
    for r in range(replicas):
        for h in range(grad.shape[1] // TILE):
            pay[r, sub + h * rows : sub + (h + 1) * rows, :] = grad_b[
                r * rows : (r + 1) * rows, h * TILE : (h + 1) * TILE
            ]


def dense_call(parts, features, scale_col, scale_row, weight, bias, cotangent):
    sub, width = features.shape
    replicas = parts.shape[0]
    hid = weight.shape[1]
    extra = width // replicas * (hid // TILE)
    return pl.pallas_call(
        dense_kernel,
        in_specs=[vmem()] * 7,
        out_specs=(vmem(), vmem(), vmem()),
        out_shape=(
            jax.ShapeDtypeStruct((sub, hid), BF16),
            jax.ShapeDtypeStruct((sub, width), BF16),
            jax.ShapeDtypeStruct((replicas, sub + extra, width), BF16),
        ),
        compiler_params=pltpu.CompilerParams(vmem_limit_bytes=VMEM_BYTES),
        name="dense",
    )(parts, features, scale_col, scale_row, weight, bias, cotangent)


def backward_kernel(group, core, rows, cols, count, tiles, back, near, far, grad):
    step = pl.program_id(0)
    mine = core[0]
    sub = 2 * TILE
    replicas, height, width = back.shape

    @pl.when(step == 0)
    def _():
        grad[...] = jnp.sum(back[:, sub:, :].astype(F32), axis=0).astype(BF16)

    for b in range(group):
        for half, target in enumerate((near, far)):
            which = mine if half == 0 else 1 - mine
            first = b * 2 * SLOTS + which * SLOTS
            block = (step * group + b) * 2 + which
            live = count[0, block]
            pieces = []
            for s in range(SLOTS):
                column = cols[0, block * SLOTS + s]
                row = rows[0, block * SLOTS + s]
                used = s < live
                tile = back[row // 2, pl.ds(pl.multiple_of((row % 2) * TILE, TILE), TILE), :]
                blank = jnp.zeros_like(tile)
                top = jnp.where(used & (column == 0), tile, blank)
                low = jnp.where(used & (column != 0), tile, blank)
                pieces.append(jnp.concatenate([top, low], axis=0))
            stack = tiles[pl.ds(first, SLOTS)].reshape(SLOTS * TILE, TILE)
            products = jnp.dot(
                jnp.concatenate(pieces, axis=1), stack, preferred_element_type=F32
            )
            target[b, :sub, :] = products.astype(BF16)
            target[b, sub:, :] = grad[...]


def backward_call(core, tile_rows, tile_cols, tile_count, tile_values, back, group=2):
    slots = tile_values.shape[0]
    steps = slots // (2 * SLOTS * group)
    replicas, height, width = back.shape
    out = pl.BlockSpec((group, height, width), lambda i, *_: (i, 0, 0))
    shape = jax.ShapeDtypeStruct((steps * group, height, width), BF16)
    return pl.pallas_call(
        functools.partial(backward_kernel, group),
        grid_spec=pltpu.PrefetchScalarGridSpec(
            num_scalar_prefetch=4,
            grid=(steps,),
            in_specs=[
                pl.BlockSpec((2 * SLOTS * group, TILE, TILE), lambda i, *_: (i, 0, 0)),
                pl.BlockSpec((replicas, height, width), lambda i, *_: (0, 0, 0)),
            ],
            out_specs=(out, out),
            scratch_shapes=[pltpu.VMEM((height - 2 * TILE, width), BF16)],
        ),
        out_shape=(shape, shape),
        compiler_params=params(),
        name="backward",
    )(core, tile_rows, tile_cols, tile_count, tile_values, back)


def final_kernel(parts, back_own, scale_row, grad_features, grad_piece):
    sub = back_own.shape[0]
    total = jnp.sum(parts[...].astype(F32), axis=0)
    for c in range(sub // TILE):
        here = slice(c * TILE, (c + 1) * TILE)
        value = (total[here, :] + back_own[here, :].astype(F32)) * scale_row[c : c + 1, :]
        grad_features[here, :] = value.T.astype(BF16)
    for r in range(grad_piece.shape[0]):
        grad_piece[r] = total[sub:, :]


def final_call(parts, back_own, scale_row, replicas):
    sub, width = back_own.shape
    extra = parts.shape[1] - sub
    return pl.pallas_call(
        final_kernel,
        in_specs=[vmem()] * 3,
        out_specs=(vmem(), vmem()),
        out_shape=(
            jax.ShapeDtypeStruct((sub, width), BF16),
            jax.ShapeDtypeStruct((replicas, extra, width), F32),
        ),
        compiler_params=pltpu.CompilerParams(vmem_limit_bytes=VMEM_BYTES),
        name="final",
    )(parts, back_own, scale_row)


SWAP = ((0, 1), (1, 0))


def body(features, tile_values, tile_rows, tile_cols, tile_count, weight, bias, cotangent):
    replicas = lax.axis_size("rep")
    sub, width = features.shape
    row_tiles = sub * replicas // TILE
    ring = lax.axis_size("zed") * lax.axis_size("pair")
    core = lax.axis_index("core").astype(jnp.int32).reshape(1)

    partial = degree_call(tile_rows, tile_count, tile_values, row_tiles)
    parts = lax.all_to_all(
        partial.reshape(replicas, sub // TILE, TILE), "rep", 0, 0, tiled=True
    )
    scale_row, scale_col, spread = scale_call(parts, features, ring)
    near = lax.all_to_all(spread, ("zed", "pair"), 0, 0, tiled=True)
    far = lax.ppermute(near, "core", SWAP)
    sums = forward_call(
        core, tile_rows, tile_cols, tile_count, tile_values, near, far, row_tiles
    )
    sums = lax.all_to_all(sums.reshape(replicas, sub, width), "rep", 0, 0, tiled=True)
    hidden, back_own, pay = dense_call(
        sums, features, scale_col, scale_row, weight, bias.reshape(1, -1), cotangent
    )
    back = lax.all_to_all(pay, "rep", 0, 0, tiled=True)
    near, far = backward_call(core, tile_rows, tile_cols, tile_count, tile_values, back)
    near = near + lax.ppermute(far, "core", SWAP)
    near = lax.all_to_all(near, ("zed", "pair"), 0, 0, tiled=True)
    grad_features, piece = final_call(near, back_own, scale_row, replicas)
    piece = lax.all_to_all(piece, "rep", 0, 0, tiled=True)
    hid = weight.shape[1]
    rows = width // replicas
    grad_weight = (
        piece.reshape(replicas, hid // TILE, rows, TILE)
        .transpose(0, 2, 1, 3)
        .reshape(width, hid)
    )
    return hidden, grad_features, grad_weight


def solution(mesh):
    rows, replicas = mesh.devices.shape
    fine = Mesh(
        mesh.devices.reshape(rows // 4, 2, 2, replicas), ("zed", "pair", "core", "rep")
    )
    whole = ("zed", "pair", "core", "rep")
    placed = (
        P(whole, None),
        P(whole, None, None),
        P(whole, None),
        P(whole, None),
        P(whole, None),
        P(),
        P(),
        P(whole, None),
    )
    return jax.shard_map(
        body,
        mesh=fine,
        in_specs=placed,
        out_specs=(P(whole, None), P(whole, None), P()),
        check_vma=False,
    )
```

time: 760 us -> 164 us (0.22)
  waiting for transfers between devices: 473 us -> 5.49 us
  local copies, waits for them, and re-layouts: 166 us -> 2.13 us
  blocking collectives: 23.8 us -> 125 us
  matrix products: 68.7 us -> 0 us
  Pallas kernels: 0 us -> 29.3 us
  between operations: 14 us -> 0.76 us
  other arithmetic: 11.8 us -> 0.31 us
    psum x2 -> x0, waiting for transfers between devices: 296 us -> none  [the longest x1 204 us: body(): grad_weight = lax.psum(weight_term, 'row')]
    all_to_all x0 -> x6, blocking collectives: none -> 125 us  [the longest x1 36.1 us: body(): near = lax.all_to_all(near, ('zed', 'pair'), 0, 0, tiled=True)]
    reduce_scatter x1 -> x0, waiting for transfers between devices: 115 us -> none  [body(): lax.psum_scatter(placed.reshape(lax.axis_size('row') * sub_rows, feature_...]
    gather x1 -> x0, local copies, waits for them, and re-layouts: 112 us -> none  [body(): jnp.take(segment, jnp.clip(positions, 0, length - 1).reshape(-1), axis=0)]
    dot_general x9 -> x0, matrix products: 68.7 us -> none  [the longest x1 19.4 us: body(): jnp.einsum('skt,stf->skf', part_tiles, picked, preferred_element_type=jnp...]
    all_gather x2 -> x0, waiting for transfers between devices: 61.3 us -> none  [the longest x1 61.3 us: body(): segment = lax.all_gather(scaled, 'row', axis=0, tiled=True)]
    dot_general x4 -> x0, local copies, waits for them, and re-layouts: 33.1 us -> none  [the longest x1 17.5 us: body(): jnp.einsum('skt,stf->skf', part_tiles, picked, preferred_element_type=jnp...]
    pallas_call x0 -> x6, Pallas kernels: none -> 29.3 us  [the longest x1 9.79 us: forward_call(): pl.pallas_call(functools.partial(forward_kernel, group), grid_spec=pltpu....]
  transfers between devices with their start and end apart: 5 -> 2, of which waited for: 4 -> 2; matrix products, arithmetic and copies ran while one was open for 22% -> 0% of each run, Pallas kernels for 0% -> 0%
where the time goes in v1:
time: 164 us; the launch traced here: 163 us
  blocking collectives  125 us (76%)
  Pallas kernels  29.3 us (18%)
  waiting for transfers between devices  5.49 us (3%)
  local copies, waits for them, and re-layouts  2.13 us (1%)
    all_to_all x1, blocking collectives, body(): near = lax.all_to_all(near, ('zed', 'pair'), 0, 0, tiled=True)  36.1 us
    all_to_all x1, blocking collectives, body(): near = lax.all_to_all(spread, ('zed', 'pair'), 0, 0, tiled=True)  35.2 us
    all_to_all x1, blocking collectives, body(): back = lax.all_to_all(pay, 'rep', 0, 0, tiled=True)  14.9 us
    all_to_all x1, blocking collectives, body(): lax.all_to_all(sums.reshape(replicas, sub, width), 'rep', 0, 0, tiled=True)  14.5 us
    all_to_all x1, blocking collectives, body(): lax.all_to_all(partial.reshape(replicas, sub // TILE, TILE), 'rep', 0, 0,...  13.7 us
    all_to_all x1, blocking collectives, body(): piece = lax.all_to_all(piece, 'rep', 0, 0, tiled=True)  10.5 us
    pallas_call x1, Pallas kernels, forward_call(): pl.pallas_call(functools.partial(forward_kernel, group), grid_spec=pltpu....  9.79 us
    pallas_call x1, Pallas kernels, backward_call(): pl.pallas_call(functools.partial(backward_kernel, group), grid_spec=pltpu...  9.62 us
  transfers between devices with their start and end apart: 2, of which 2 were waited for; matrix products, arithmetic and copies ran while one was open for 0% of the time, Pallas kernels for 0%

profile of v1, /device:TPU:2, one launch (start us, length us, event | category | flops | bytes accessed | tf_op | source)
XLA Modules:
  0.0 162.9 jit_solution(17610230237621709241)
XLA Ops:
  0.6 0.0 copy-start
  0.6 0.0 copy-start.3
  0.7 0.7 copy-done.3
  1.4 0.0 copy-start.5
  1.4 0.7 copy-done.5
  2.0 7.8 %degree.1 = f32[16,128]{1,0:T(8,128)S(1)} custom-call(s32[1,256]{1,0:T(1,128)S(1)} %copy-done.3, s32[1,32]{1,0:T(1,128)S(1)} %copy-done.5, bf16[256,128,128]{2,1,0:T(8,128)(2,1)} %tiles.5), custom_call_target="tpu_custom_call" | custom-call | tf_op jit(solution)/shard_map/degree/pallas_call | solution.py:55
  9.8 0.0 copy-start.4
  9.8 0.0 copy-start.6
  9.8 0.0 copy-start.7
  9.9 13.7 %all_to_all.30.parts = f32[8,2,128]{2,1,0:T(2,128)S(1)} all-to-all(f32[8,2,128]{2,1,0:T(2,128)S(1)} %bitcast.13), channel_id=1, replica_groups=mesh['zed'=8,'pair'=2,'core'=2,'rep'=8] {'rep'}, dimensions={0} | all-to-all | bytes 16384 | tf_op jit(solution)/shard_map/all_to_all | solution.py:306
  23.5 0.0 copy-done
  23.5 0.2 scale.1
  23.7 35.2 %all_to_all.31.near = bf16[16,256,128]{2,1,0:T(8,128)(2,1)S(1)} all-to-all(bf16[16,256,128]{2,1,0:T(8,128)(2,1)S(1)} %get-tuple-element.13), channel_id=1, replica_groups=mesh['zed'=8,'pair'=2,'core'=2,'rep'=8] {'zed','pair'}, dimensions={0} | all-to-all | bytes 2097152 | tf_op jit(solution)/shard_map/all_to_all | solution.py:310
  58.9 0.0 collective-permute-start
  58.9 2.7 %collective-permute-done.far = bf16[16,256,128]{2,1,0:T(8,128)(2,1)S(1)} collective-permute-done((bf16[16,256,128]{2,1,0:T(8,128)(2,1)S(1)}, bf16[16,256,128]{2,1,0:T(8,128)(2,1)S(1)}, u32[]{:S(2)}, u32[]{:S(2)}) %collective-permute-start) | collective-permute-done | bytes 1048608 | tf_op jit(solution)/shard_map/ppermute | solution.py:311
  61.6 0.0 copy-done.4
  61.6 0.0 copy-done.6
  61.6 0.0 copy-done.7
  61.6 0.0 copy-start.1
  61.6 0.0 copy-start.2
  61.6 0.0 copy-start.8
  61.6 9.8 %forward.1 = bf16[16,128,128]{2,1,0:T(8,128)(2,1)S(1)} custom-call(s32[1]{0:T(128)} %bitcast.core, s32[1,256]{1,0:T(1,128)S(1)} %copy-done.4, s32[1,256]{1,0:T(1,128)S(1)} %copy-done.7, s32[1,32]{1,0:T(1,128)S(1)} %copy-done.6, bf16[256,128,128]{2,1,0:T(8,128)(2,1)} %tiles.5, bf16[16,256,128]{2,1,0:T(8,128)(2,1)S(1)} %all_to_all.31.near, ...), custom_call_target="tpu_custom_call" | custom-call | tf_op jit(solution)/shard_map/forward/pallas_call | solution.py:138
  71.4 14.5 %all_to_all.32.parts = bf16[8,256,128]{2,1,0:T(8,128)(2,1)S(1)} all-to-all(bf16[8,256,128]{2,1,0:T(8,128)(2,1)S(1)} %bitcast.12), channel_id=1, replica_groups=mesh['zed'=8,'pair'=2,'core'=2,'rep'=8] {'rep'}, dimensions={0} | all-to-all | bytes 1048576 | tf_op jit(solution)/shard_map/all_to_all | solution.py:315
  85.9 0.0 copy-done.1
  85.9 0.0 copy-done.2
  85.9 0.0 copy-done.8
  85.9 1.0 dense.1
  87.0 14.9 %all_to_all.33.back = bf16[8,288,128]{2,1,0:T(8,128)(2,1)S(1)} all-to-all(bf16[8,288,128]{2,1,0:T(8,128)(2,1)S(1)} %get-tuple-element.17), channel_id=1, replica_groups=mesh['zed'=8,'pair'=2,'core'=2,'rep'=8] {'rep'}, dimensions={0} | all-to-all | bytes 1179648 | tf_op jit(solution)/shard_map/all_to_all | solution.py:319
  101.9 9.6 %backward.1 = (bf16[16,288,128]{2,1,0:T(8,128)(2,1)S(1)}, bf16[16,288,128]{2,1,0:T(8,128)(2,1)S(1)}) custom-call(s32[1]{0:T(128)} %bitcast.core, s32[1,256]{1,0:T(1,128)S(1)} %copy-done.4, s32[1,256]{1,0:T(1,128)S(1)} %copy-done.7, s32[1,32]{1,0:T(1,128)S(1)} %copy-done.6, bf16[256,128,128]{2,1,0:T(8,128)(2,1)} %tiles.5, ...), custom_call_target="tpu_custom_call" | custom-call | tf_op jit(solution)/shard_map/backward/pallas_call | solution.py:250
  111.6 0.1 collective-permute-start.1
  111.7 2.8 %collective-permute-done.1 = bf16[16,288,128]{2,1,0:T(8,128)(2,1)S(1)} collective-permute-done((bf16[16,288,128]{2,1,0:T(8,128)(2,1)S(1)}, bf16[16,288,128]{2,1,0:T(8,128)(2,1)S(1)}, u32[]{:S(2)}, u32[]{:S(2)}) %collective-permute-start.1) | collective-permute-done | bytes 1179680 | tf_op jit(solution)/shard_map/ppermute | solution.py:321
  114.5 0.3 add.3
  114.8 36.1 %all_to_all.34.parts = bf16[16,288,128]{2,1,0:T(8,128)(2,1)S(1)} all-to-all(bf16[16,288,128]{2,1,0:T(8,128)(2,1)S(1)} %add.3), channel_id=1, replica_groups=mesh['zed'=8,'pair'=2,'core'=2,'rep'=8] {'zed','pair'}, dimensions={0} | all-to-all | bytes 2359296 | tf_op jit(solution)/shard_map/all_to_all | solution.py:322
  150.9 0.9 final.1
  151.7 10.5 %all_to_all.35 = f32[8,32,128]{2,1,0:T(8,128)S(1)} all-to-all(f32[8,32,128]{2,1,0:T(8,128)S(1)} %get-tuple-element.22), channel_id=1, replica_groups=mesh['zed'=8,'pair'=2,'core'=2,'rep'=8] {'rep'}, dimensions={0} | all-to-all | bytes 262144 | tf_op jit(solution)/shard_map/all_to_all | solution.py:324
  162.2 0.1 copy.11
  162.3 0.7 copy.14
Async XLA Ops:
  0.6 22.9 %copy-start = (bf16[256,128]{1,0:T(8,128)(2,1)S(1)}, bf16[256,128]{1,0:T(8,128)(2,1)}, u32[]{:S(2)}) copy-start(bf16[256,128]{1,0:T(8,128)(2,1)} %features.3) | copy-start | bytes 196612
  0.6 0.7 copy-start.3
  1.4 0.7 copy-start.5
  9.8 51.7 %copy-start.4 = (s32[1,256]{1,0:T(1,128)S(1)}, s32[1,256]{1,0:T(1,128)}, u32[]{:S(2)}) copy-start(s32[1,256]{1,0:T(1,128)} %rows.5) | copy-start | bytes 3076
  9.8 51.7 %copy-start.6 = (s32[1,32]{1,0:T(1,128)S(1)}, s32[1,32]{1,0:T(1,128)}, u32[]{:S(2)}) copy-start(s32[1,32]{1,0:T(1,128)} %count.5) | copy-start | bytes 388
  9.8 51.7 %copy-start.7 = (s32[1,256]{1,0:T(1,128)S(1)}, s32[1,256]{1,0:T(1,128)}, u32[]{:S(2)}) copy-start(s32[1,256]{1,0:T(1,128)} %cols.3) | copy-start | bytes 3076
  58.9 2.7 %collective-permute-start = (bf16[16,256,128]{2,1,0:T(8,128)(2,1)S(1)}, bf16[16,256,128]{2,1,0:T(8,128)(2,1)S(1)}, u32[]{:S(2)}, u32[]{:S(2)}) collective-permute-start(bf16[16,256,128]{2,1,0:T(8,128)(2,1)S(1)} %all_to_all.31.near), channel_id=1, source_target_pairs={{0,8},{8,0},{1,9},{9,1},{2,10},{10,2},{3,11},{11,3},{4,12},{12,4},... | collective-permute-start | bytes 3145736 | tf_op jit(solution)/shard_map/ppermute | solution.py:311
  61.6 24.4 %copy-start.1 = (bf16[256,256]{1,0:T(8,128)(2,1)S(1)}, bf16[256,256]{1,0:T(8,128)(2,1)}, u32[]{:S(2)}) copy-start(bf16[256,256]{1,0:T(8,128)(2,1)} %cotangent.1) | copy-start | bytes 393220
  61.6 24.4 %copy-start.2 = (bf16[128,256]{1,0:T(8,128)(2,1)S(1)}, bf16[128,256]{1,0:T(8,128)(2,1)}, u32[]{:S(2)}) copy-start(bf16[128,256]{1,0:T(8,128)(2,1)} %weight.1) | copy-start | bytes 196612
  61.6 24.3 %copy-start.8 = (f32[256]{0:T(256)S(1)}, f32[256]{0:T(256)}, u32[]{:S(2)}) copy-start(f32[256]{0:T(256)} %param.14) | copy-start | bytes 3076
  111.6 2.9 %collective-permute-start.1 = (bf16[16,288,128]{2,1,0:T(8,128)(2,1)S(1)}, bf16[16,288,128]{2,1,0:T(8,128)(2,1)S(1)}, u32[]{:S(2)}, u32[]{:S(2)}) collective-permute-start(bf16[16,288,128]{2,1,0:T(8,128)(2,1)S(1)} %get-tuple-element.19), channel_id=1, source_target_pairs={{0,8},{8,0},{1,9},{9,1},{2,10},{10,2},{3,11},{11,3},{4,12},{12,4},... | collective-permute-start | bytes 3538952 | tf_op jit(solution)/shard_map/ppermute | solution.py:321

commit v2 on v1

v2 whole, which is shorter than its diff:
```python
import functools

import jax
import jax.numpy as jnp
from jax import lax
from jax.experimental import pallas as pl
from jax.experimental.pallas import tpu as pltpu
from jax.sharding import Mesh, PartitionSpec as P

TILE = 128
SLOTS = 8
BF16 = jnp.bfloat16
F32 = jnp.float32
VMEM_BYTES = 16 * 1024 * 1024
DEGREE_BYTES = 50 * 1024 * 1024
REACH = 4


def params():
    return pltpu.CompilerParams(vmem_limit_bytes=VMEM_BYTES)


def vmem():
    return pl.BlockSpec(memory_space=pltpu.VMEM)


def smem():
    return pl.BlockSpec(memory_space=pltpu.SMEM)


def lookup(meta):
    slots = (meta.shape[1] - 3) * SLOTS // (2 * SLOTS + 1)
    blocks = slots // SLOTS

    def rows(slot):
        return meta[0, slot]

    def cols(slot):
        return meta[0, slots + slot]

    def count(block):
        return meta[0, 2 * slots + block]

    def place(axis):
        return meta[0, 2 * slots + blocks + axis]

    return rows, cols, count, place


def degree_kernel(chunks, meta, tiles, out, held, acc, sems):
    rows, _, count, _ = lookup(meta)
    row_tiles = out.shape[0]
    size = tiles.shape[0] // chunks
    copies = [
        pltpu.make_async_copy(
            tiles.at[pl.ds(c * size, size)], held.at[pl.ds(c * size, size)], sems.at[c]
        )
        for c in range(chunks)
    ]
    for copy in copies:
        copy.start()
    acc[...] = jnp.zeros_like(acc)
    ones = jnp.ones((16, TILE), BF16)
    for c in range(chunks):
        copies[c].wait()
        for block in range(c * size // SLOTS, (c + 1) * size // SLOTS):
            live = count(block)
            stack = held[block * SLOTS : (block + 1) * SLOTS].reshape(SLOTS * TILE, TILE)
            sums = lax.dot_general(
                ones, stack, (((1,), (1,)), ((), ())), preferred_element_type=F32
            )
            for s in range(SLOTS):
                row = jnp.where(s < live, rows(block * SLOTS + s), row_tiles)
                acc[row] += sums[:8, s * TILE : (s + 1) * TILE]
    for r in range(row_tiles):
        out[r : r + 1, :] = acc[r, 0:1, :]


def degree_call(meta, tiles, row_tiles, chunks=4):
    return pl.pallas_call(
        functools.partial(degree_kernel, chunks),
        in_specs=[smem(), pl.BlockSpec(memory_space=pl.ANY)],
        out_specs=vmem(),
        out_shape=jax.ShapeDtypeStruct((row_tiles, TILE), F32),
        scratch_shapes=[
            pltpu.VMEM(tiles.shape, BF16),
            pltpu.VMEM((row_tiles + 1, 8, TILE), F32),
            pltpu.SemaphoreType.DMA((chunks,)),
        ],
        compiler_params=pltpu.CompilerParams(vmem_limit_bytes=DEGREE_BYTES),
        name="degree",
    )(meta, tiles)


def join_kernel(one, two, three, four, out, half):
    for i, piece in enumerate((one, two, three, four)):
        out[i] = piece[...]
        if i < 2:
            half[i] = piece[...]


def join_call(*pieces):
    shape = pieces[0].shape
    return pl.pallas_call(
        join_kernel,
        in_specs=[vmem()] * 4,
        out_specs=(vmem(), vmem()),
        out_shape=(
            jax.ShapeDtypeStruct((4,) + shape, BF16),
            jax.ShapeDtypeStruct((2,) + shape, BF16),
        ),
        compiler_params=params(),
        name="join",
    )(*pieces)


def scale_kernel(parts, row_out, col_out, spread):
    degree = 1.0 + jnp.sum(parts[...], axis=0)
    scale = lax.rsqrt(degree)
    row_out[...] = scale
    for c in range(scale.shape[0]):
        here = slice(c * TILE, (c + 1) * TILE)
        col_out[here, :] = jnp.broadcast_to(scale[c : c + 1, :], (TILE, TILE)).T
    spread[...] = jnp.broadcast_to(scale[None], spread.shape)


def scale_call(parts, copies):
    halves = parts.shape[1]
    return pl.pallas_call(
        scale_kernel,
        in_specs=[vmem()],
        out_specs=(vmem(), vmem(), vmem()),
        out_shape=(
            jax.ShapeDtypeStruct((halves, TILE), F32),
            jax.ShapeDtypeStruct((halves * TILE, TILE), F32),
            jax.ShapeDtypeStruct((copies, halves, TILE), F32),
        ),
        compiler_params=params(),
        name="scale",
    )(parts)


def block_of(place, core, length, ahead, a, b):
    there = lax.rem(place(0) + ahead + length, length)
    return there * 4 + (place(1) ^ a) * 2 + (core ^ b)


def forward_kernel(length, first, meta, tiles, scales, *refs):
    rows, cols, count, place = lookup(meta)
    core = place(2)
    sign = 1 - 2 * core
    if first:
        sources, (out, scaled) = refs[:-2], refs[-2:]
        acc = out
        work = [(sources[0], i, core, 0) for i in range(4)]
        for k in range(1, REACH + 1):
            work += [(sources[k], i, core, -sign * k) for i in range(sources[k].shape[0])]
    else:
        before, sources, (out, scaled, acc) = refs[0], refs[1:-3], refs[-3:]
        work = []
        for k in range(1, REACH + 1):
            piece = sources[k - 1]
            work += [(piece, i, 1 - core, sign * k) for i in range(piece.shape[0])]
    row_tiles = acc.shape[0] - 1
    acc[...] = jnp.zeros_like(acc)
    for n, (source, i, side, ahead) in enumerate(work):
        block = block_of(place, side, length, ahead, i % 2, i // 2)
        live = count(block)
        for c in range(2):
            column = jnp.broadcast_to(scales[block, c : c + 1, :], (TILE, TILE)).T
            plain = source[i, c * TILE : (c + 1) * TILE, :].astype(F32)
            scaled[n, c] = (column * plain).astype(BF16)
        for s in range(SLOTS):
            slot = block * SLOTS + s
            product = jnp.dot(
                tiles[slot], scaled[n, cols(slot)], preferred_element_type=F32
            )
            row = jnp.where(s < live, rows(slot), row_tiles)
            acc[row] += product
    if not first:
        out[...] = (before[:row_tiles] + acc[:row_tiles]).astype(BF16)


def forward_call(length, meta, tiles, scales, before, sources, row_tiles):
    blocks = scales.shape[0]
    width = sources[0].shape[2]
    first = before is None
    total = (row_tiles + 1, TILE, width)
    given = list(sources) if first else [before, *sources]
    scratch = [pltpu.VMEM((blocks, 2, TILE, width), BF16)]
    if first:
        shape = jax.ShapeDtypeStruct(total, F32)
    else:
        shape = jax.ShapeDtypeStruct((row_tiles, TILE, width), BF16)
        scratch.append(pltpu.VMEM(total, F32))
    return pl.pallas_call(
        functools.partial(forward_kernel, length, first),
        in_specs=[smem()] + [vmem()] * (2 + len(given)),
        out_specs=vmem(),
        out_shape=shape,
        scratch_shapes=scratch,
        compiler_params=params(),
        name="forward_near" if first else "forward_far",
    )(meta, tiles, scales, *given)


def dense_kernel(parts, features, scale_col, scale_row, weight, bias, cotangent, hidden, back_own, pay):
    sub = features.shape[0]
    replicas = parts.shape[0]
    column = scale_col[...]
    total = (column * features[...].astype(F32)).astype(BF16).astype(F32)
    for r in range(replicas):
        total += parts[r].astype(F32)
    agg_b = (column * total).astype(BF16)
    w = weight[...]
    v = jnp.dot(agg_b, w, preferred_element_type=F32) + bias[...]
    root = 0.7978845608028654
    square = v * v
    t = jnp.tanh(root * (v + 0.044715 * (square * v)))
    cdf = 0.5 * (1.0 + t)
    hidden[...] = (v * cdf).astype(BF16)
    slope = cdf + 0.5 * v * ((1.0 - t) * (1.0 + t)) * (root * (1.0 + (3 * 0.044715) * square))
    dpre = (cotangent[...].astype(F32) * slope).astype(BF16)
    grad = lax.dot_general(agg_b, dpre, (((0,), (0,)), ((), ())), preferred_element_type=F32)
    back = lax.dot_general(w, dpre, (((1,), (1,)), ((), ())), preferred_element_type=F32)
    for c in range(sub // TILE):
        here = slice(c * TILE, (c + 1) * TILE)
        piece = (back[:, here] * scale_row[c : c + 1, :]).astype(BF16)
        back_own[here, :] = piece
        for r in range(replicas):
            pay[r, here, :] = piece
    grad_b = grad.astype(BF16)
    rows = grad.shape[0] // replicas
    for r in range(replicas):
        for h in range(grad.shape[1] // TILE):
            pay[r, sub + h * rows : sub + (h + 1) * rows, :] = grad_b[
                r * rows : (r + 1) * rows, h * TILE : (h + 1) * TILE
            ]


def dense_call(parts, features, scale_col, scale_row, weight, bias, cotangent):
    sub, width = features.shape
    replicas = parts.shape[0]
    hid = weight.shape[1]
    extra = width // replicas * (hid // TILE)
    return pl.pallas_call(
        dense_kernel,
        in_specs=[vmem()] * 7,
        out_specs=(vmem(), vmem(), vmem()),
        out_shape=(
            jax.ShapeDtypeStruct((sub, hid), BF16),
            jax.ShapeDtypeStruct((sub, width), BF16),
            jax.ShapeDtypeStruct((replicas, sub + extra, width), BF16),
        ),
        compiler_params=params(),
        name="dense",
    )(parts, features, scale_col, scale_row, weight, bias, cotangent)


def backward_kernel(length, mine, meta, tiles, back, *outs):
    rows, cols, count, place = lookup(meta)
    side = place(2) if mine else 1 - place(2)
    sign = 1 - 2 * side
    for a in (1, 0):
        work = [(sign * k, b) for k in range(1, REACH) for b in range(2)]
        work += [(REACH, 0), (0, 0)]
        for n, (ahead, b) in enumerate(work):
            block = block_of(place, side, length, ahead, a, b)
            live = count(block)
            low = jnp.zeros((TILE, TILE), F32)
            high = low
            for s in range(SLOTS):
                slot = block * SLOTS + s
                row = rows(slot)
                column = cols(slot)
                used = s < live
                tile = back[row // 2, pl.ds(pl.multiple_of((row % 2) * TILE, TILE), TILE), :]
                product = jnp.dot(tile, tiles[slot], preferred_element_type=F32)
                low += jnp.where(used & (column == 0), product, 0.0)
                high += jnp.where(used & (column != 0), product, 0.0)
            outs[a][n, :TILE] = low.astype(BF16)
            outs[a][n, TILE:] = high.astype(BF16)
    if len(outs) == 3:
        piece = jnp.sum(back[:, 2 * TILE :, :].astype(F32), axis=0).astype(BF16)
        for r in range(outs[2].shape[0]):
            outs[2][r] = piece


def backward_call(length, mine, meta, tiles, back):
    height, width = back.shape[1:]
    blocks = tiles.shape[0] // SLOTS
    shapes = [jax.ShapeDtypeStruct((length, 2 * TILE, width), BF16)] * 2
    if mine:
        shapes.append(jax.ShapeDtypeStruct((blocks, height - 2 * TILE, width), BF16))
    return pl.pallas_call(
        functools.partial(backward_kernel, length, mine),
        in_specs=[smem()] + [vmem()] * 2,
        out_specs=(vmem(),) * len(shapes),
        out_shape=tuple(shapes),
        compiler_params=params(),
        name="backward_near" if mine else "backward_far",
    )(meta, tiles, back)


def grad_kernel(parts, out):
    out[...] = jnp.broadcast_to(jnp.sum(parts[...].astype(F32), axis=0)[None], out.shape)


def grad_call(parts, replicas):
    return pl.pallas_call(
        grad_kernel,
        in_specs=[vmem()],
        out_specs=vmem(),
        out_shape=jax.ShapeDtypeStruct((replicas,) + parts.shape[1:], F32),
        compiler_params=params(),
        name="grad",
    )(parts)


def fold_kernel(one, two, three, four, own, keep, give):
    total = one[...].astype(F32) + two[...].astype(F32) + three[...].astype(F32)
    keep[...] = total[0] + four[0].astype(F32) + own[0].astype(F32)
    give[...] = total[1].astype(BF16)


def fold_call(parts, own):
    shape = own.shape[1:]
    return pl.pallas_call(
        fold_kernel,
        in_specs=[vmem()] * 5,
        out_specs=(vmem(), vmem()),
        out_shape=(jax.ShapeDtypeStruct(shape, F32), jax.ShapeDtypeStruct(shape, BF16)),
        compiler_params=params(),
        name="fold",
    )(*parts, own)


def final_kernel(keep, got, back_own, scale_row, pieces, grad_features, grad_weight):
    for c in range(back_own.shape[0] // TILE):
        here = slice(c * TILE, (c + 1) * TILE)
        value = keep[here, :] + got[here, :].astype(F32) + back_own[here, :].astype(F32)
        grad_features[here, :] = (value * scale_row[c : c + 1, :]).T.astype(BF16)
    replicas, height, width = pieces.shape
    halves = grad_weight.shape[1] // width
    rows = height // halves
    for r in range(replicas):
        for h in range(halves):
            grad_weight[r * rows : (r + 1) * rows, h * width : (h + 1) * width] = pieces[
                r, h * rows : (h + 1) * rows, :
            ]


def final_call(keep, got, back_own, scale_row, pieces):
    replicas, height, width = pieces.shape
    return pl.pallas_call(
        final_kernel,
        in_specs=[vmem()] * 5,
        out_specs=(vmem(), vmem()),
        out_shape=(
            jax.ShapeDtypeStruct(back_own.shape, BF16),
            jax.ShapeDtypeStruct((TILE, replicas * height * width // TILE), F32),
        ),
        compiler_params=params(),
        name="final",
    )(keep, got, back_own, scale_row, pieces)


SWAP = ((0, 1), (1, 0))


def body(features, tile_values, tile_rows, tile_cols, tile_count, weight, bias, cotangent):
    replicas = lax.axis_size("rep")
    length = lax.axis_size("zed")
    blocks = tile_count.shape[1]
    sub, width = features.shape
    row_tiles = sub * replicas // TILE
    place = [lax.axis_index(n).astype(jnp.int32).reshape(1, 1) for n in ("zed", "pair", "core")]
    meta = jnp.concatenate([tile_rows, tile_cols, tile_count, *place], axis=1)

    def along(value, k):
        moves = [
            (z * 2 + c, (z + (1 - 2 * c) * k) % length * 2 + c)
            for z in range(length)
            for c in range(2)
        ]
        return lax.ppermute(value, ("zed", "core"), moves)

    def swap(value, axis):
        return lax.ppermute(value, axis, SWAP)

    partner = swap(features, "pair")
    sibling = swap(features, "core")
    partial = degree_call(meta, tile_values, row_tiles)
    partner, partial = lax.optimization_barrier((partner, partial))
    own, two = join_call(features, partner, sibling, swap(partner, "core"))
    own, two, partial = lax.optimization_barrier((own, two, partial))
    near = [along(own if k < REACH else two, k) for k in range(1, REACH + 1)]
    parts = lax.all_to_all(
        partial.reshape(replicas, sub // TILE, TILE), "rep", 0, 0, tiled=True
    )
    scale_row, scale_col, spread = scale_call(parts, blocks)
    scales = lax.all_to_all(spread, ("zed", "pair", "core"), 0, 0, tiled=True)
    scales, near = lax.optimization_barrier((scales, near))
    far = [swap(value, "core") for value in near]
    sums = forward_call(length, meta, tile_values, scales, None, [own, *near], row_tiles)
    sums = forward_call(length, meta, tile_values, scales, sums, far, row_tiles)
    sums = lax.all_to_all(sums.reshape(replicas, sub, width), "rep", 0, 0, tiled=True)
    hidden, back_own, pay = dense_call(
        sums, features, scale_col, scale_row, weight, bias.reshape(1, -1), cotangent
    )
    back = lax.all_to_all(pay, "rep", 0, 0, tiled=True)

    far = backward_call(length, False, meta, tile_values, back)
    far = [swap(far[1], "core"), swap(far[0], "core")]
    *near, piece = backward_call(length, True, meta, tile_values, back)
    other = swap(near[1] + far[0], "pair")
    mine = near[0] + far[1]

    piece = lax.all_to_all(piece, ("zed", "pair", "core"), 0, 0, tiled=True)
    mine = mine + other
    parts = [
        along(mine[2 * k - 2 : 2 * k] if k < REACH else mine[2 * k - 2 : 2 * k - 1], k)
        for k in range(1, REACH + 1)
    ]
    piece = lax.all_to_all(grad_call(piece, replicas), "rep", 0, 0, tiled=True)
    keep, give = fold_call(parts, mine[2 * REACH - 1 :])
    grad_features, grad_weight = final_call(
        keep, swap(give, "core"), back_own, scale_row, piece
    )
    return hidden, grad_features, grad_weight


def solution(mesh):
    rows, replicas = mesh.devices.shape
    fine = Mesh(
        mesh.devices.reshape(rows // 4, 2, 2, replicas), ("zed", "pair", "core", "rep")
    )
    whole = ("zed", "pair", "core", "rep")
    placed = (
        P(whole, None),
        P(whole, None, None),
        P(whole, None),
        P(whole, None),
        P(whole, None),
        P(),
        P(),
        P(whole, None),
    )
    return jax.shard_map(
        body,
        mesh=fine,
        in_specs=placed,
        out_specs=(P(whole, None), P(whole, None), P()),
        check_vma=False,
    )
```

time: 164 us -> 129 us (0.79)
  blocking collectives: 125 us -> 59.2 us
  starting transfers between devices: 0.1 us -> 28.9 us
  waiting for transfers between devices: 5.49 us -> 19.7 us
  Pallas kernels: 29.3 us -> 18.9 us
    all_to_all x3 -> x1, blocking collectives: 81.7 us -> 15.8 us  [body(): scales = lax.all_to_all(spread, ('zed', 'pair', 'core'), 0, 0, tiled=True)]
    ppermute x2 -> x19, starting transfers between devices: 0.1 us -> 21 us  [the longest x8 15.1 us: along(): return lax.ppermute(value, ('zed', 'core'), moves)]
    pallas_call x5 -> x10, Pallas kernels: 28.3 us -> 17.8 us  [the longest x2 5.55 us: backward_call(): pl.pallas_call(functools.partial(backward_kernel, length, mine), in_specs...]
    ppermute x2 -> x19, waiting for transfers between devices: 5.49 us -> 15.3 us  [the longest x11 11.8 us: swap(): return lax.ppermute(value, axis, SWAP)]
    all_to_all x0 -> x2, starting transfers between devices: none -> 7.83 us  [the longest x1 4.46 us: body(): piece = lax.all_to_all(piece, ('zed', 'pair', 'core'), 0, 0, tiled=True)]
    all_to_all x0 -> x2, waiting for transfers between devices: none -> 4.36 us  [the longest x1 4.36 us: body(): piece = lax.all_to_all(grad_call(piece, replicas), 'rep', 0, 0, tiled=True)]
    unnamed x19 -> x10, local copies, waits for them, and re-layouts: 2.07 us -> 0.03 us
  transfers between devices with their start and end apart: 2 -> 21, of which waited for: 2 -> 5; matrix products, arithmetic and copies ran while one was open for 0% -> 1% of each run, Pallas kernels for 0% -> 9%
where the time goes in v2:
time: 129 us; the launch traced here: 128 us
  blocking collectives  59.2 us (46%)
  starting transfers between devices  28.9 us (22%)
  waiting for transfers between devices  19.7 us (15%)
  Pallas kernels  18.9 us (15%)
    all_to_all x1, blocking collectives, body(): scales = lax.all_to_all(spread, ('zed', 'pair', 'core'), 0, 0, tiled=True)  15.8 us
    all_to_all x1, blocking collectives, body(): back = lax.all_to_all(pay, 'rep', 0, 0, tiled=True)  15.2 us
    ppermute x8, starting transfers between devices, along(): return lax.ppermute(value, ('zed', 'core'), moves)  15.1 us
    all_to_all x1, blocking collectives, body(): lax.all_to_all(sums.reshape(replicas, sub, width), 'rep', 0, 0, tiled=True)  14.4 us
    all_to_all x1, blocking collectives, body(): lax.all_to_all(partial.reshape(replicas, sub // TILE, TILE), 'rep', 0, 0,...  13.8 us
    ppermute x11, waiting for transfers between devices, swap(): return lax.ppermute(value, axis, SWAP)  11.8 us
    ppermute x11, starting transfers between devices, swap(): return lax.ppermute(value, axis, SWAP)  5.91 us
    pallas_call x2, Pallas kernels, backward_call(): pl.pallas_call(functools.partial(backward_kernel, length, mine), in_specs...  5.55 us
  transfers between devices with their start and end apart: 21, of which 5 were waited for; matrix products, arithmetic and copies ran while one was open for 1% of the time, Pallas kernels for 9%

profile of v2, /device:TPU:2, one launch (start us, length us, event | category | flops | bytes accessed | tf_op | source)
XLA Modules:
  0.0 128.5 jit_solution(13778785914680983117)
XLA Ops:
  0.6 2.4 %collective-permute-start = (bf16[256,128]{1,0:T(8,128)(2,1)}, bf16[256,128]{1,0:T(8,128)(2,1)S(1)}, u32[]{:S(2)}, u32[]{:S(2)}) collective-permute-start(bf16[256,128]{1,0:T(8,128)(2,1)} %features.1), channel_id=1, source_target_pairs={{0,16},{16,0},{1,17},{17,1},{2,18},{18,2},{3,19},{19,3},{4,20},{20... | collective-permute-start | bytes 196616 | tf_op jit(solution)/shard_map/ppermute | solution.py:389
  3.0 0.0 collective-permute-start.1
  3.0 0.8 concatenate.3.meta
  3.8 5.3 %degree.1 = f32[16,128]{1,0:T(8,128)S(1)} custom-call(s32[1,547]{1,0:T(1,128)S(1)} %concatenate.3.meta, bf16[256,128,128]{2,1,0:T(8,128)(2,1)} %tiles.9), custom_call_target="tpu_custom_call" | custom-call | tf_op jit(solution)/shard_map/degree/pallas_call | solution.py:80
  9.1 0.0 collective-permute-done.two
  9.1 0.6 collective-permute-start.2
  9.7 0.0 collective-permute-done.1.three
  9.7 0.9 collective-permute-done.2.four
  10.6 0.0 copy-done.1
  10.6 0.3 collective-permute-start.3
  11.0 3.2 %collective-permute-start.4 = (bf16[4,256,128]{2,1,0:T(8,128)(2,1)S(1)}, bf16[4,256,128]{2,1,0:T(8,128)(2,1)S(1)}, u32[]{:S(2)}, u32[]{:S(2)}) collective-permute-start(bf16[4,256,128]{2,1,0:T(8,128)(2,1)S(1)} %get-tuple-element.36.refs_0_), channel_id=1, source_target_pairs={{0,64},{8,200},{32,96},{40,232},{64,128},{72,8},{96,160},{104,40},... | collective-permute-start | bytes 786440 | tf_op jit(solution)/shard_map/ppermute | solution.py:386
  14.2 3.9 %collective-permute-start.5 = (bf16[4,256,128]{2,1,0:T(8,128)(2,1)S(1)}, bf16[4,256,128]{2,1,0:T(8,128)(2,1)S(1)}, u32[]{:S(2)}, u32[]{:S(2)}) collective-permute-start(bf16[4,256,128]{2,1,0:T(8,128)(2,1)S(1)} %get-tuple-element.36.refs_0_), channel_id=1, source_target_pairs={{0,96},{8,168},{32,128},{40,200},{64,160},{72,232},{96,192},{104,8... | collective-permute-start | bytes 786440 | tf_op jit(solution)/shard_map/ppermute | solution.py:386
  18.1 0.7 collective-permute-start.6
  18.8 13.8 %all_to_all.30.parts = f32[8,2,128]{2,1,0:T(2,128)S(1)} all-to-all(f32[8,2,128]{2,1,0:T(2,128)S(1)} %bitcast.7), channel_id=1, replica_groups=mesh['zed'=8,'pair'=2,'core'=2,'rep'=8] {'rep'}, dimensions={0} | all-to-all | bytes 16384 | tf_op jit(solution)/shard_map/all_to_all | solution.py:398
  32.6 0.1 scale.1
  32.7 15.8 %all_to_all.31.scales = f32[32,2,128]{2,1,0:T(2,128)S(1)} all-to-all(f32[32,2,128]{2,1,0:T(2,128)S(1)} %get-tuple-element.35), channel_id=1, replica_groups=mesh['zed'=8,'pair'=2,'core'=2,'rep'=8] {'zed','pair','core'}, dimensions={0} | all-to-all | bytes 65536 | tf_op jit(solution)/shard_map/all_to_all | solution.py:402
  48.5 0.0 collective-permute-done.6.refs_4_
  48.5 0.0 collective-permute-done.3.refs_1_
  48.5 0.0 collective-permute-done.4.refs_2_
  48.5 0.0 collective-permute-done.5.refs_3_
  48.5 0.1 collective-permute-start.7
  48.6 0.5 collective-permute-start.8
  49.1 0.1 collective-permute-start.9
  49.2 0.4 collective-permute-start.10
  49.6 2.8 %forward_near.1.refs_0_ = f32[17,128,128]{2,1,0:T(8,128)S(1)} custom-call(s32[1,547]{1,0:T(1,128)S(1)} %concatenate.3.meta, bf16[256,128,128]{2,1,0:T(8,128)(2,1)S(1)} %copy-done, f32[32,2,128]{2,1,0:T(2,128)S(1)} %all_to_all.31.scales, bf16[4,256,128]{2,1,0:T(8,128)(2,1)S(1)} %get-tuple-element.36.refs_0_, ...), custom_call_target="tpu_custom_call" | custom-call | tf_op jit(solution)/shard_map/forward_near/pallas_call | solution.py:196
  52.5 0.0 copy-start.2
  52.5 0.0 copy-start.3
  52.5 0.0 copy-start.4
  52.5 0.0 collective-permute-done.10.refs_4_
  52.5 0.0 collective-permute-done.7.refs_1_
  52.5 0.0 collective-permute-done.8.refs_2_
  52.5 0.0 collective-permute-done.9.refs_3_
  52.6 2.5 %forward_far.1 = bf16[16,128,128]{2,1,0:T(8,128)(2,1)S(1)} custom-call(s32[1,547]{1,0:T(1,128)S(1)} %concatenate.3.meta, bf16[256,128,128]{2,1,0:T(8,128)(2,1)S(1)} %copy-done, f32[32,2,128]{2,1,0:T(2,128)S(1)} %all_to_all.31.scales, f32[17,128,128]{2,1,0:T(8,128)S(1)} %forward_near.1.refs_0_, bf16[4,256,128]{2,1,0:T(8,128)(2,1)S(1)} %collective-permute-done.7.refs_1_, ...), custom_call_target="tpu_custom_call" | custom-call | tf_op jit(solution)/shard_map/forward_far/pallas_call | solution.py:196
  55.0 14.4 %all_to_all.32.parts = bf16[8,256,128]{2,1,0:T(8,128)(2,1)S(1)} all-to-all(bf16[8,256,128]{2,1,0:T(8,128)(2,1)S(1)} %bitcast.6), channel_id=1, replica_groups=mesh['zed'=8,'pair'=2,'core'=2,'rep'=8] {'rep'}, dimensions={0} | all-to-all | bytes 1048576 | tf_op jit(solution)/shard_map/all_to_all | solution.py:407
  69.4 0.0 copy-done.2
  69.5 1.1 dense.1
  70.5 15.2 %all_to_all.33.back = bf16[8,288,128]{2,1,0:T(8,128)(2,1)S(1)} all-to-all(bf16[8,288,128]{2,1,0:T(8,128)(2,1)S(1)} %get-tuple-element.46), channel_id=1, replica_groups=mesh['zed'=8,'pair'=2,'core'=2,'rep'=8] {'rep'}, dimensions={0} | all-to-all | bytes 1179648 | tf_op jit(solution)/shard_map/all_to_all | solution.py:411
  85.7 2.4 %backward_far.1 = (bf16[8,256,128]{2,1,0:T(8,128)(2,1)S(1)}, bf16[8,256,128]{2,1,0:T(8,128)(2,1)S(1)}) custom-call(s32[1,547]{1,0:T(1,128)S(1)} %concatenate.3.meta, bf16[256,128,128]{2,1,0:T(8,128)(2,1)S(1)} %copy-done, bf16[8,288,128]{2,1,0:T(8,128)(2,1)S(1)} %all_to_all.33.back), custom_call_target="tpu_custom_call" | custom-call | tf_op jit(solution)/shard_map/backward_far/pallas_call | solution.py:295
  88.1 0.1 collective-permute-start.12
  88.2 0.5 collective-permute-start.11
  88.7 3.1 %backward_near.1 = (bf16[8,256,128]{2,1,0:T(8,128)(2,1)S(1)}, bf16[8,256,128]{2,1,0:T(8,128)(2,1)S(1)}, bf16[32,32,128]{2,1,0:T(8,128)(2,1)}) custom-call(s32[1,547]{1,0:T(1,128)S(1)} %concatenate.3.meta, bf16[256,128,128]{2,1,0:T(8,128)(2,1)S(1)} %copy-done, bf16[8,288,128]{2,1,0:T(8,128)(2,1)S(1)} %all_to_all.33.back), custom_call_target="tpu_custom_call" | custom-call | tf_op jit(solution)/shard_map/backward_near/pallas_call | solution.py:295
  91.8 0.0 collective-permute-done.12
  91.8 0.1 add.10
  92.0 1.2 collective-permute-start.13
  93.2 4.5 %all-to-all-start.4 = ((bf16[32,32,128]{2,1,0:T(8,128)(2,1)}), bf16[32,32,128]{2,1,0:T(8,128)(2,1)S(1)}, u32[]{:S(2)}, u32[]{:S(2)}) async-start(bf16[32,32,128]{2,1,0:T(8,128)(2,1)} %get-tuple-element.54), calls=%async_computation.4 | async-start | bytes 524288 | tf_op jit(solution)/shard_map/all_to_all | solution.py:419
  97.6 0.0 collective-permute-done.11
  97.6 10.9 %collective-permute-done.13 = bf16[8,256,128]{2,1,0:T(8,128)(2,1)S(1)} collective-permute-done((bf16[8,256,128]{2,1,0:T(8,128)(2,1)S(1)}, bf16[8,256,128]{2,1,0:T(8,128)(2,1)S(1)}, u32[]{:S(2)}, u32[]{:S(2)}) %collective-permute-start.13) | collective-permute-done | bytes 524320 | tf_op jit(solution)/shard_map/ppermute | solution.py:389
  108.5 0.1 add_add_fusion
  108.7 0.6 collective-permute-start.14
  109.3 0.0 collective-permute-start.15
  109.3 2.9 %collective-permute-start.16 = (bf16[2,256,128]{2,1,0:T(8,128)(2,1)S(1)}, bf16[2,256,128]{2,1,0:T(8,128)(2,1)S(1)}, u32[]{:S(2)}, u32[]{:S(2)}) collective-permute-start(bf16[2,256,128]{2,1,0:T(8,128)(2,1)S(1)} %get-tuple-element.59), channel_id=1, source_target_pairs={{0,96},{8,168},{32,128},{40,200},{64,160},{72,232},{96,192},{104,8... | collective-permute-start | bytes 393224 | tf_op jit(solution)/shard_map/ppermute | solution.py:386
  112.2 3.4 %collective-permute-start.17 = (bf16[1,256,128]{2,1,0:T(8,128)(2,1)S(1)}, bf16[1,256,128]{2,1,0:T(8,128)(2,1)S(1)}, u32[]{:S(2)}, u32[]{:S(2)}) collective-permute-start(bf16[1,256,128]{2,1,0:T(8,128)(2,1)S(1)} %get-tuple-element.58), channel_id=1, source_target_pairs={{0,128},{8,136},{32,160},{40,168},{64,192},{72,200},{96,224},{104,... | collective-permute-start | bytes 196616 | tf_op jit(solution)/shard_map/ppermute | solution.py:386
  115.6 0.0 all-to-all-done.4.parts
  115.6 0.7 grad.1
  116.3 3.4 %all-to-all-start.5 = ((f32[8,32,128]{2,1,0:T(8,128)}), f32[8,32,128]{2,1,0:T(8,128)S(1)}, u32[]{:S(2)}, u32[]{:S(2)}) async-start(f32[8,32,128]{2,1,0:T(8,128)} %grad.1), calls=%async_computation.5 | async-start | bytes 262144 | tf_op jit(solution)/shard_map/all_to_all | solution.py:425
  119.7 2.4 %collective-permute-done.17.four = bf16[1,256,128]{2,1,0:T(8,128)(2,1)S(1)} collective-permute-done((bf16[1,256,128]{2,1,0:T(8,128)(2,1)S(1)}, bf16[1,256,128]{2,1,0:T(8,128)(2,1)S(1)}, u32[]{:S(2)}, u32[]{:S(2)}) %collective-permute-start.17) | collective-permute-done | bytes 65568 | tf_op jit(solution)/shard_map/ppermute | solution.py:386
  122.1 0.0 collective-permute-done.14.one
  122.1 0.0 collective-permute-done.15.two
  122.1 1.1 collective-permute-done.16.three
  123.2 0.1 fold.1
  123.3 0.1 collective-permute-start.18
  123.4 4.4 %all-to-all-done.5.pieces = f32[8,32,128]{2,1,0:T(8,128)S(1)} async-done(((f32[8,32,128]{2,1,0:T(8,128)}), f32[8,32,128]{2,1,0:T(8,128)S(1)}, u32[]{:S(2)}, u32[]{:S(2)}) %all-to-all-start.5) | async-done | bytes 131104 | tf_op jit(solution)/shard_map/all_to_all | solution.py:425
  127.7 0.0 collective-permute-done.18.got
  127.7 0.7 final.1
  (8 shorter events, 0.1 us)
Async XLA Ops:
  0.6 10.0 %copy-start.1 = (bf16[256,128]{1,0:T(8,128)(2,1)S(1)}, bf16[256,128]{1,0:T(8,128)(2,1)}, u32[]{:S(2)}) copy-start(bf16[256,128]{1,0:T(8,128)(2,1)} %features.1) | copy-start | bytes 196612
  0.6 8.4 %collective-permute-start = (bf16[256,128]{1,0:T(8,128)(2,1)}, bf16[256,128]{1,0:T(8,128)(2,1)S(1)}, u32[]{:S(2)}, u32[]{:S(2)}) collective-permute-start(bf16[256,128]{1,0:T(8,128)(2,1)} %features.1), channel_id=1, source_target_pairs={{0,16},{16,0},{1,17},{17,1},{2,18},{18,2},{3,19},{19,3},{4,20},{20... | collective-permute-start | bytes 196616 | tf_op jit(solution)/shard_map/ppermute | solution.py:389
  3.0 6.7 %collective-permute-start.1 = (bf16[256,128]{1,0:T(8,128)(2,1)}, bf16[256,128]{1,0:T(8,128)(2,1)S(1)}, u32[]{:S(2)}, u32[]{:S(2)}) collective-permute-start(bf16[256,128]{1,0:T(8,128)(2,1)} %features.1), channel_id=1, source_target_pairs={{0,8},{8,0},{1,9},{9,1},{2,10},{10,2},{3,11},{11,3},{4,12},{12,4},... | collective-permute-start | bytes 196616 | tf_op jit(solution)/shard_map/ppermute | solution.py:389
  3.8 45.9 %copy-start = (bf16[256,128,128]{2,1,0:T(8,128)(2,1)S(1)}, bf16[256,128,128]{2,1,0:T(8,128)(2,1)}, u32[]{:S(2)}) copy-start(bf16[256,128,128]{2,1,0:T(8,128)(2,1)} %tiles.9) | copy-start | bytes 25165828
  9.1 1.5 %collective-permute-start.2 = (bf16[256,128]{1,0:T(8,128)(2,1)S(1)}, bf16[256,128]{1,0:T(8,128)(2,1)S(1)}, u32[]{:S(2)}, u32[]{:S(2)}) collective-permute-start(bf16[256,128]{1,0:T(8,128)(2,1)S(1)} %collective-permute-done.two), channel_id=1, source_target_pairs={{0,8},{8,0},{1,9},{9,1},{2,10},{10,2},{3,11},{11,3},{4,12},{12,4},... | collective-permute-start | bytes 196616 | tf_op jit(solution)/shard_map/ppermute | solution.py:389
  10.6 37.9 %collective-permute-start.3 = (bf16[4,256,128]{2,1,0:T(8,128)(2,1)S(1)}, bf16[4,256,128]{2,1,0:T(8,128)(2,1)S(1)}, u32[]{:S(2)}, u32[]{:S(2)}) collective-permute-start(bf16[4,256,128]{2,1,0:T(8,128)(2,1)S(1)} %get-tuple-element.36.refs_0_), channel_id=1, source_target_pairs={{0,32},{8,232},{32,64},{40,8},{64,96},{72,40},{96,128},{104,72},{1... | collective-permute-start | bytes 786440 | tf_op jit(solution)/shard_map/ppermute | solution.py:386
  11.0 37.6 %collective-permute-start.4 = (bf16[4,256,128]{2,1,0:T(8,128)(2,1)S(1)}, bf16[4,256,128]{2,1,0:T(8,128)(2,1)S(1)}, u32[]{:S(2)}, u32[]{:S(2)}) collective-permute-start(bf16[4,256,128]{2,1,0:T(8,128)(2,1)S(1)} %get-tuple-element.36.refs_0_), channel_id=1, source_target_pairs={{0,64},{8,200},{32,96},{40,232},{64,128},{72,8},{96,160},{104,40},... | collective-permute-start | bytes 786440 | tf_op jit(solution)/shard_map/ppermute | solution.py:386
  14.2 34.3 %collective-permute-start.5 = (bf16[4,256,128]{2,1,0:T(8,128)(2,1)S(1)}, bf16[4,256,128]{2,1,0:T(8,128)(2,1)S(1)}, u32[]{:S(2)}, u32[]{:S(2)}) collective-permute-start(bf16[4,256,128]{2,1,0:T(8,128)(2,1)S(1)} %get-tuple-element.36.refs_0_), channel_id=1, source_target_pairs={{0,96},{8,168},{32,128},{40,200},{64,160},{72,232},{96,192},{104,8... | collective-permute-start | bytes 786440 | tf_op jit(solution)/shard_map/ppermute | solution.py:386
  18.1 30.4 %collective-permute-start.6 = (bf16[2,256,128]{2,1,0:T(8,128)(2,1)S(1)}, bf16[2,256,128]{2,1,0:T(8,128)(2,1)S(1)}, u32[]{:S(2)}, u32[]{:S(2)}) collective-permute-start(bf16[2,256,128]{2,1,0:T(8,128)(2,1)S(1)} %get-tuple-element.37), channel_id=1, source_target_pairs={{0,128},{8,136},{32,160},{40,168},{64,192},{72,200},{96,224},{104,... | collective-permute-start | bytes 393224 | tf_op jit(solution)/shard_map/ppermute | solution.py:386
  48.5 4.0 %collective-permute-start.7 = (bf16[4,256,128]{2,1,0:T(8,128)(2,1)S(1)}, bf16[4,256,128]{2,1,0:T(8,128)(2,1)S(1)}, u32[]{:S(2)}, u32[]{:S(2)}) collective-permute-start(bf16[4,256,128]{2,1,0:T(8,128)(2,1)S(1)} %collective-permute-done.3.refs_1_), channel_id=1, source_target_pairs={{0,8},{8,0},{1,9},{9,1},{2,10},{10,2},{3,11},{11,3},{4,12},{12,4},... | collective-permute-start | bytes 786440 | tf_op jit(solution)/shard_map/ppermute | solution.py:389
  48.6 3.9 %collective-permute-start.8 = (bf16[4,256,128]{2,1,0:T(8,128)(2,1)S(1)}, bf16[4,256,128]{2,1,0:T(8,128)(2,1)S(1)}, u32[]{:S(2)}, u32[]{:S(2)}) collective-permute-start(bf16[4,256,128]{2,1,0:T(8,128)(2,1)S(1)} %collective-permute-done.4.refs_2_), channel_id=1, source_target_pairs={{0,8},{8,0},{1,9},{9,1},{2,10},{10,2},{3,11},{11,3},{4,12},{12,4},... | collective-permute-start | bytes 786440 | tf_op jit(solution)/shard_map/ppermute | solution.py:389
  49.1 3.4 %collective-permute-start.9 = (bf16[4,256,128]{2,1,0:T(8,128)(2,1)S(1)}, bf16[4,256,128]{2,1,0:T(8,128)(2,1)S(1)}, u32[]{:S(2)}, u32[]{:S(2)}) collective-permute-start(bf16[4,256,128]{2,1,0:T(8,128)(2,1)S(1)} %collective-permute-done.5.refs_3_), channel_id=1, source_target_pairs={{0,8},{8,0},{1,9},{9,1},{2,10},{10,2},{3,11},{11,3},{4,12},{12,4},... | collective-permute-start | bytes 786440 | tf_op jit(solution)/shard_map/ppermute | solution.py:389
  49.2 3.3 %collective-permute-start.10 = (bf16[2,256,128]{2,1,0:T(8,128)(2,1)S(1)}, bf16[2,256,128]{2,1,0:T(8,128)(2,1)S(1)}, u32[]{:S(2)}, u32[]{:S(2)}) collective-permute-start(bf16[2,256,128]{2,1,0:T(8,128)(2,1)S(1)} %collective-permute-done.6.refs_4_), channel_id=1, source_target_pairs={{0,8},{8,0},{1,9},{9,1},{2,10},{10,2},{3,11},{11,3},{4,12},{12,4},... | collective-permute-start | bytes 393224 | tf_op jit(solution)/shard_map/ppermute | solution.py:389
  52.5 17.0 %copy-start.2 = (bf16[256,256]{1,0:T(8,128)(2,1)S(1)}, bf16[256,256]{1,0:T(8,128)(2,1)}, u32[]{:S(2)}) copy-start(bf16[256,256]{1,0:T(8,128)(2,1)} %cotangent.1) | copy-start | bytes 393220
  52.5 17.0 %copy-start.3 = (bf16[128,256]{1,0:T(8,128)(2,1)S(1)}, bf16[128,256]{1,0:T(8,128)(2,1)}, u32[]{:S(2)}) copy-start(bf16[128,256]{1,0:T(8,128)(2,1)} %weight.1) | copy-start | bytes 196612
  52.5 17.0 %copy-start.4 = (f32[256]{0:T(256)S(1)}, f32[256]{0:T(256)}, u32[]{:S(2)}) copy-start(f32[256]{0:T(256)} %param.14) | copy-start | bytes 3076
  88.1 3.7 %collective-permute-start.12 = (bf16[8,256,128]{2,1,0:T(8,128)(2,1)S(1)}, bf16[8,256,128]{2,1,0:T(8,128)(2,1)S(1)}, u32[]{:S(2)}, u32[]{:S(2)}) collective-permute-start(bf16[8,256,128]{2,1,0:T(8,128)(2,1)S(1)} %get-tuple-element.50), channel_id=1, source_target_pairs={{0,8},{8,0},{1,9},{9,1},{2,10},{10,2},{3,11},{11,3},{4,12},{12,4},... | collective-permute-start | bytes 1572872 | tf_op jit(solution)/shard_map/ppermute | solution.py:389
  88.2 9.4 %collective-permute-start.11 = (bf16[8,256,128]{2,1,0:T(8,128)(2,1)S(1)}, bf16[8,256,128]{2,1,0:T(8,128)(2,1)S(1)}, u32[]{:S(2)}, u32[]{:S(2)}) collective-permute-start(bf16[8,256,128]{2,1,0:T(8,128)(2,1)S(1)} %get-tuple-element.48), channel_id=1, source_target_pairs={{0,8},{8,0},{1,9},{9,1},{2,10},{10,2},{3,11},{11,3},{4,12},{12,4},... | collective-permute-start | bytes 1572872 | tf_op jit(solution)/shard_map/ppermute | solution.py:389
  92.0 16.6 %collective-permute-start.13 = (bf16[8,256,128]{2,1,0:T(8,128)(2,1)S(1)}, bf16[8,256,128]{2,1,0:T(8,128)(2,1)S(1)}, u32[]{:S(2)}, u32[]{:S(2)}) collective-permute-start(bf16[8,256,128]{2,1,0:T(8,128)(2,1)S(1)} %add.10), channel_id=1, source_target_pairs={{0,16},{16,0},{1,17},{17,1},{2,18},{18,2},{3,19},{19,3},{4,20},{20... | collective-permute-start | bytes 1572872 | tf_op jit(solution)/shard_map/ppermute | solution.py:389
  93.2 22.5 %all-to-all-start.4 = ((bf16[32,32,128]{2,1,0:T(8,128)(2,1)}), bf16[32,32,128]{2,1,0:T(8,128)(2,1)S(1)}, u32[]{:S(2)}, u32[]{:S(2)}) async-start(bf16[32,32,128]{2,1,0:T(8,128)(2,1)} %get-tuple-element.54), calls=%async_computation.4 | async-start | bytes 524288 | tf_op jit(solution)/shard_map/all_to_all | solution.py:419
  108.7 13.4 %collective-permute-start.14 = (bf16[2,256,128]{2,1,0:T(8,128)(2,1)S(1)}, bf16[2,256,128]{2,1,0:T(8,128)(2,1)S(1)}, u32[]{:S(2)}, u32[]{:S(2)}) collective-permute-start(bf16[2,256,128]{2,1,0:T(8,128)(2,1)S(1)} %get-tuple-element.61), channel_id=1, source_target_pairs={{0,32},{8,232},{32,64},{40,8},{64,96},{72,40},{96,128},{104,72},{1... | collective-permute-start | bytes 393224 | tf_op jit(solution)/shard_map/ppermute | solution.py:386
  109.3 12.8 %collective-permute-start.15 = (bf16[2,256,128]{2,1,0:T(8,128)(2,1)S(1)}, bf16[2,256,128]{2,1,0:T(8,128)(2,1)S(1)}, u32[]{:S(2)}, u32[]{:S(2)}) collective-permute-start(bf16[2,256,128]{2,1,0:T(8,128)(2,1)S(1)} %get-tuple-element.60), channel_id=1, source_target_pairs={{0,64},{8,200},{32,96},{40,232},{64,128},{72,8},{96,160},{104,40},... | collective-permute-start | bytes 393224 | tf_op jit(solution)/shard_map/ppermute | solution.py:386
  109.3 13.9 %collective-permute-start.16 = (bf16[2,256,128]{2,1,0:T(8,128)(2,1)S(1)}, bf16[2,256,128]{2,1,0:T(8,128)(2,1)S(1)}, u32[]{:S(2)}, u32[]{:S(2)}) collective-permute-start(bf16[2,256,128]{2,1,0:T(8,128)(2,1)S(1)} %get-tuple-element.59), channel_id=1, source_target_pairs={{0,96},{8,168},{32,128},{40,200},{64,160},{72,232},{96,192},{104,8... | collective-permute-start | bytes 393224 | tf_op jit(solution)/shard_map/ppermute | solution.py:386
  112.2 9.9 %collective-permute-start.17 = (bf16[1,256,128]{2,1,0:T(8,128)(2,1)S(1)}, bf16[1,256,128]{2,1,0:T(8,128)(2,1)S(1)}, u32[]{:S(2)}, u32[]{:S(2)}) collective-permute-start(bf16[1,256,128]{2,1,0:T(8,128)(2,1)S(1)} %get-tuple-element.58), channel_id=1, source_target_pairs={{0,128},{8,136},{32,160},{40,168},{64,192},{72,200},{96,224},{104,... | collective-permute-start | bytes 196616 | tf_op jit(solution)/shard_map/ppermute | solution.py:386
  116.3 11.4 %all-to-all-start.5 = ((f32[8,32,128]{2,1,0:T(8,128)}), f32[8,32,128]{2,1,0:T(8,128)S(1)}, u32[]{:S(2)}, u32[]{:S(2)}) async-start(f32[8,32,128]{2,1,0:T(8,128)} %grad.1), calls=%async_computation.5 | async-start | bytes 262144 | tf_op jit(solution)/shard_map/all_to_all | solution.py:425
  123.3 4.5 %collective-permute-start.18 = (bf16[256,128]{1,0:T(8,128)(2,1)S(1)}, bf16[256,128]{1,0:T(8,128)(2,1)S(1)}, u32[]{:S(2)}, u32[]{:S(2)}) collective-permute-start(bf16[256,128]{1,0:T(8,128)(2,1)S(1)} %get-tuple-element.52), channel_id=1, source_target_pairs={{0,8},{8,0},{1,9},{9,1},{2,10},{10,2},{3,11},{11,3},{4,12},{12,4},... | collective-permute-start | bytes 196616 | tf_op jit(solution)/shard_map/ppermute | solution.py:389

commit v3 on v2

--- a/solution.py
+++ b/solution.py
@@ -257,15 +257,18 @@
     )(parts, features, scale_col, scale_row, weight, bias, cotangent)
 
 
+LONG = ((3, 0), (3, 1), (2, 0), (2, 1))
+SHORT = ((1, 0), (1, 1), (4, 0), (0, 0))
+
+
 def backward_kernel(length, mine, meta, tiles, back, *outs):
     rows, cols, count, place = lookup(meta)
     side = place(2) if mine else 1 - place(2)
     sign = 1 - 2 * side
-    for a in (1, 0):
-        work = [(sign * k, b) for k in range(1, REACH) for b in range(2)]
-        work += [(REACH, 0), (0, 0)]
-        for n, (ahead, b) in enumerate(work):
-            block = block_of(place, side, length, ahead, a, b)
+    plan = ((LONG, 1), (SHORT, 1), (LONG, 0), (SHORT, 0))
+    for out, (group, a) in zip(outs, plan):
+        for n, (k, b) in enumerate(group):
+            block = block_of(place, side, length, sign * k, a, b)
             live = count(block)
             low = jnp.zeros((TILE, TILE), F32)
             high = low
@@ -278,18 +281,18 @@
                 product = jnp.dot(tile, tiles[slot], preferred_element_type=F32)
                 low += jnp.where(used & (column == 0), product, 0.0)
                 high += jnp.where(used & (column != 0), product, 0.0)
-            outs[a][n, :TILE] = low.astype(BF16)
-            outs[a][n, TILE:] = high.astype(BF16)
-    if len(outs) == 3:
+            out[n, :TILE] = low.astype(BF16)
+            out[n, TILE:] = high.astype(BF16)
+    if mine:
         piece = jnp.sum(back[:, 2 * TILE :, :].astype(F32), axis=0).astype(BF16)
-        for r in range(outs[2].shape[0]):
-            outs[2][r] = piece
+        for r in range(outs[4].shape[0]):
+            outs[4][r] = piece
 
 
 def backward_call(length, mine, meta, tiles, back):
     height, width = back.shape[1:]
     blocks = tiles.shape[0] // SLOTS
-    shapes = [jax.ShapeDtypeStruct((length, 2 * TILE, width), BF16)] * 2
+    shapes = [jax.ShapeDtypeStruct((len(LONG), 2 * TILE, width), BF16)] * 4
     if mine:
         shapes.append(jax.ShapeDtypeStruct((blocks, height - 2 * TILE, width), BF16))
     return pl.pallas_call(
@@ -411,19 +414,20 @@
     back = lax.all_to_all(pay, "rep", 0, 0, tiled=True)
 
     far = backward_call(length, False, meta, tile_values, back)
-    far = [swap(far[1], "core"), swap(far[0], "core")]
+    far = [swap(value, "core") for value in far]
     *near, piece = backward_call(length, True, meta, tile_values, back)
-    other = swap(near[1] + far[0], "pair")
-    mine = near[0] + far[1]
-
+    sums = [n + f for n, f in zip(near, far)]
+    sums[0], sums[1], piece = lax.optimization_barrier((sums[0], sums[1], piece))
+    other = [swap(value, "pair") for value in sums[:2]]
     piece = lax.all_to_all(piece, ("zed", "pair", "core"), 0, 0, tiled=True)
-    mine = mine + other
-    parts = [
-        along(mine[2 * k - 2 : 2 * k] if k < REACH else mine[2 * k - 2 : 2 * k - 1], k)
-        for k in range(1, REACH + 1)
-    ]
-    piece = lax.all_to_all(grad_call(piece, replicas), "rep", 0, 0, tiled=True)
-    keep, give = fold_call(parts, mine[2 * REACH - 1 :])
+    piece = grad_call(piece, replicas)
+    reach = sums[2] + other[0]
+    three, two = along(reach[:2], 3), along(reach[2:], 2)
+    other[1], piece = lax.optimization_barrier((other[1], piece))
+    piece = lax.all_to_all(piece, "rep", 0, 0, tiled=True)
+    close = sums[3] + other[1]
+    one, four = along(close[:2], 1), along(close[2:3], 4)
+    keep, give = fold_call((one, two, three, four), close[3:])
     grad_features, grad_weight = final_call(
         keep, swap(give, "core"), back_own, scale_row, piece
     )

time: 129 us -> 127 us (0.984)
  waiting for transfers between devices: 19.7 us -> 16.9 us
    ppermute x11 -> x14, waiting for transfers between devices: 11.8 us -> 4.12 us  [swap(): return lax.ppermute(value, axis, SWAP)]
    all_to_all x1, waiting for transfers between devices: 0.01 us -> 4.91 us  [body(): piece = lax.all_to_all(piece, ('zed', 'pair', 'core'), 0, 0, tiled=True)]
    ppermute x11 -> x14, starting transfers between devices: 5.91 us -> 6.56 us  [swap(): return lax.ppermute(value, axis, SWAP)]
  transfers between devices with their start and end apart: 21 -> 24, of which waited for: 5 -> 5; matrix products, arithmetic and copies ran while one was open for 1% -> 1% of each run, Pallas kernels for 9% -> 10%
where the time goes in v3:
time: 127 us
  blocking collectives  59.1 us (47%)
  starting transfers between devices  29.9 us (24%)
  Pallas kernels  18.9 us (15%)
  waiting for transfers between devices  16.9 us (13%)
    all_to_all x1, blocking collectives, body(): scales = lax.all_to_all(spread, ('zed', 'pair', 'core'), 0, 0, tiled=True)  15.7 us
    ppermute x8, starting transfers between devices, along(): return lax.ppermute(value, ('zed', 'core'), moves)  15.5 us
    all_to_all x1, blocking collectives, body(): back = lax.all_to_all(pay, 'rep', 0, 0, tiled=True)  15.2 us
    all_to_all x1, blocking collectives, body(): lax.all_to_all(sums.reshape(replicas, sub, width), 'rep', 0, 0, tiled=True)  14.4 us
    all_to_all x1, blocking collectives, body(): lax.all_to_all(partial.reshape(replicas, sub // TILE, TILE), 'rep', 0, 0,...  13.8 us
    ppermute x14, starting transfers between devices, swap(): return lax.ppermute(value, axis, SWAP)  6.56 us
    pallas_call x2, Pallas kernels, backward_call(): pl.pallas_call(functools.partial(backward_kernel, length, mine), in_specs...  5.6 us
    pallas_call x1, Pallas kernels, degree_call(): pl.pallas_call(functools.partial(degree_kernel, chunks), in_specs=[smem()...  5.31 us
  transfers between devices with their start and end apart: 24, of which 5 were waited for; matrix products, arithmetic and copies ran while one was open for 1% of the time, Pallas kernels for 10%

profile of v3, /device:TPU:2, one launch (start us, length us, event | category | flops | bytes accessed | tf_op | source)
XLA Modules:
  0.0 126.8 jit_solution(9797802799779505059)
XLA Ops:
  0.6 2.4 %collective-permute-start = (bf16[256,128]{1,0:T(8,128)(2,1)}, bf16[256,128]{1,0:T(8,128)(2,1)S(1)}, u32[]{:S(2)}, u32[]{:S(2)}) collective-permute-start(bf16[256,128]{1,0:T(8,128)(2,1)} %features.1), channel_id=1, source_target_pairs={{0,16},{16,0},{1,17},{17,1},{2,18},{18,2},{3,19},{19,3},{4,20},{20... | collective-permute-start | bytes 196616 | tf_op jit(solution)/shard_map/ppermute | solution.py:392
  3.0 0.8 concatenate.3.meta
  3.8 5.3 %degree.1 = f32[16,128]{1,0:T(8,128)S(1)} custom-call(s32[1,547]{1,0:T(1,128)S(1)} %concatenate.3.meta, bf16[256,128,128]{2,1,0:T(8,128)(2,1)} %tiles.9), custom_call_target="tpu_custom_call" | custom-call | tf_op jit(solution)/shard_map/degree/pallas_call | solution.py:80
  9.1 0.6 collective-permute-start.2
  9.7 0.0 collective-permute-done.1.three
  9.7 0.9 collective-permute-done.2.four
  10.7 0.2 collective-permute-start.3
  10.9 3.3 %collective-permute-start.4 = (bf16[4,256,128]{2,1,0:T(8,128)(2,1)S(1)}, bf16[4,256,128]{2,1,0:T(8,128)(2,1)S(1)}, u32[]{:S(2)}, u32[]{:S(2)}) collective-permute-start(bf16[4,256,128]{2,1,0:T(8,128)(2,1)S(1)} %get-tuple-element.45.refs_0_), channel_id=1, source_target_pairs={{0,64},{8,200},{32,96},{40,232},{64,128},{72,8},{96,160},{104,40},... | collective-permute-start | bytes 786440 | tf_op jit(solution)/shard_map/ppermute | solution.py:389
  14.1 4.1 %collective-permute-start.5 = (bf16[4,256,128]{2,1,0:T(8,128)(2,1)S(1)}, bf16[4,256,128]{2,1,0:T(8,128)(2,1)S(1)}, u32[]{:S(2)}, u32[]{:S(2)}) collective-permute-start(bf16[4,256,128]{2,1,0:T(8,128)(2,1)S(1)} %get-tuple-element.45.refs_0_), channel_id=1, source_target_pairs={{0,96},{8,168},{32,128},{40,200},{64,160},{72,232},{96,192},{104,8... | collective-permute-start | bytes 786440 | tf_op jit(solution)/shard_map/ppermute | solution.py:389
  18.2 0.6 collective-permute-start.6
  18.8 13.8 %all_to_all.30.parts = f32[8,2,128]{2,1,0:T(2,128)S(1)} all-to-all(f32[8,2,128]{2,1,0:T(2,128)S(1)} %bitcast.7), channel_id=1, replica_groups=mesh['zed'=8,'pair'=2,'core'=2,'rep'=8] {'rep'}, dimensions={0} | all-to-all | bytes 16384 | tf_op jit(solution)/shard_map/all_to_all | solution.py:401
  32.6 0.1 scale.1
  32.7 15.7 %all_to_all.31.scales = f32[32,2,128]{2,1,0:T(2,128)S(1)} all-to-all(f32[32,2,128]{2,1,0:T(2,128)S(1)} %get-tuple-element.44), channel_id=1, replica_groups=mesh['zed'=8,'pair'=2,'core'=2,'rep'=8] {'zed','pair','core'}, dimensions={0} | all-to-all | bytes 65536 | tf_op jit(solution)/shard_map/all_to_all | solution.py:405
  48.4 0.0 collective-permute-done.6.refs_4_
  48.4 0.0 collective-permute-done.3.refs_1_
  48.4 0.0 collective-permute-done.4.refs_2_
  48.4 0.0 collective-permute-done.5.refs_3_
  48.4 0.1 collective-permute-start.7
  48.5 0.5 collective-permute-start.8
  49.0 0.1 collective-permute-start.9
  49.1 0.4 collective-permute-start.10
  49.6 2.8 %forward_near.1.refs_0_ = f32[17,128,128]{2,1,0:T(8,128)S(1)} custom-call(s32[1,547]{1,0:T(1,128)S(1)} %concatenate.3.meta, bf16[256,128,128]{2,1,0:T(8,128)(2,1)S(1)} %copy-done, f32[32,2,128]{2,1,0:T(2,128)S(1)} %all_to_all.31.scales, bf16[4,256,128]{2,1,0:T(8,128)(2,1)S(1)} %get-tuple-element.45.refs_0_, ...), custom_call_target="tpu_custom_call" | custom-call | tf_op jit(solution)/shard_map/forward_near/pallas_call | solution.py:196
  52.4 0.0 copy-start.2
  52.4 0.0 copy-start.3
  52.4 0.0 copy-start.4
  52.4 0.0 collective-permute-done.10.refs_4_
  52.4 0.0 collective-permute-done.8.refs_2_
  52.4 0.0 collective-permute-done.9.refs_3_
  52.5 2.5 %forward_far.1 = bf16[16,128,128]{2,1,0:T(8,128)(2,1)S(1)} custom-call(s32[1,547]{1,0:T(1,128)S(1)} %concatenate.3.meta, bf16[256,128,128]{2,1,0:T(8,128)(2,1)S(1)} %copy-done, f32[32,2,128]{2,1,0:T(2,128)S(1)} %all_to_all.31.scales, f32[17,128,128]{2,1,0:T(8,128)S(1)} %forward_near.1.refs_0_, bf16[4,256,128]{2,1,0:T(8,128)(2,1)S(1)} %collective-permute-done.7.refs_1_, ...), custom_call_target="tpu_custom_call" | custom-call | tf_op jit(solution)/shard_map/forward_far/pallas_call | solution.py:196
  54.9 14.4 %all_to_all.32.parts = bf16[8,256,128]{2,1,0:T(8,128)(2,1)S(1)} all-to-all(bf16[8,256,128]{2,1,0:T(8,128)(2,1)S(1)} %bitcast.6), channel_id=1, replica_groups=mesh['zed'=8,'pair'=2,'core'=2,'rep'=8] {'rep'}, dimensions={0} | all-to-all | bytes 1048576 | tf_op jit(solution)/shard_map/all_to_all | solution.py:410
  69.4 1.1 dense.1
  70.4 15.2 %all_to_all.33.back = bf16[8,288,128]{2,1,0:T(8,128)(2,1)S(1)} all-to-all(bf16[8,288,128]{2,1,0:T(8,128)(2,1)S(1)} %get-tuple-element.55), channel_id=1, replica_groups=mesh['zed'=8,'pair'=2,'core'=2,'rep'=8] {'rep'}, dimensions={0} | all-to-all | bytes 1179648 | tf_op jit(solution)/shard_map/all_to_all | solution.py:414
  85.6 2.4 %backward_far.1 = (bf16[4,256,128]{2,1,0:T(8,128)(2,1)S(1)}, bf16[4,256,128]{2,1,0:T(8,128)(2,1)S(1)}, bf16[4,256,128]{2,1,0:T(8,128)(2,1)S(1)}, bf16[4,256,128]{2,1,0:T(8,128)(2,1)S(1)}) custom-call(s32[1,547]{1,0:T(1,128)S(1)} %concatenate.3.meta, bf16[256,128,128]{2,1,0:T(8,128)(2,1)S(1)} %copy-done, bf16[8,288,128]{2,1,0:T(8,128)(2,1)S(1)} %all_to_all.33.back), custom_call_target="tpu_custom_call" | custom-call | tf_op jit(solution)/shard_map/backward_far/pallas_call | solution.py:298
  88.0 0.1 collective-permute-start.13
  88.1 0.5 collective-permute-start.12
  88.6 0.1 collective-permute-start.16
  88.7 3.2 %backward_near.1 = (bf16[4,256,128]{2,1,0:T(8,128)(2,1)S(1)}, bf16[4,256,128]{2,1,0:T(8,128)(2,1)S(1)}, bf16[4,256,128]{2,1,0:T(8,128)(2,1)S(1)}, bf16[4,256,128]{2,1,0:T(8,128)(2,1)S(1)}, bf16[32,32,128]{2,1,0:T(8,128)(2,1)}) custom-call(s32[1,547]{1,0:T(1,128)S(1)} %concatenate.3.meta, bf16[256,128,128]{2,1,0:T(8,128)(2,1)S(1)} %copy-done, ...), custom_call_target="tpu_custom_call" | custom-call | tf_op jit(solution)/shard_map/backward_near/pallas_call | solution.py:298
  91.9 0.0 collective-permute-done.13
  91.9 0.1 add.20
  92.0 0.1 add.19
  92.1 1.1 collective-permute-start.17
  93.2 4.5 %all-to-all-start.4 = ((bf16[32,32,128]{2,1,0:T(8,128)(2,1)}), bf16[32,32,128]{2,1,0:T(8,128)(2,1)S(1)}, u32[]{:S(2)}, u32[]{:S(2)}) async-start(bf16[32,32,128]{2,1,0:T(8,128)(2,1)} %get-tuple-element.64), calls=%async_computation.4 | async-start | bytes 524288 | tf_op jit(solution)/shard_map/all_to_all | solution.py:422
  97.7 0.2 collective-permute-start.11
  97.9 0.4 collective-permute-start.14
  98.3 0.0 collective-permute-done.16
  98.3 3.2 %collective-permute-done.17 = bf16[4,256,128]{2,1,0:T(8,128)(2,1)S(1)} collective-permute-done((bf16[4,256,128]{2,1,0:T(8,128)(2,1)S(1)}, bf16[4,256,128]{2,1,0:T(8,128)(2,1)S(1)}, u32[]{:S(2)}, u32[]{:S(2)}) %collective-permute-start.17) | collective-permute-done | bytes 262176 | tf_op jit(solution)/shard_map/ppermute | solution.py:392
  101.5 0.1 add_add_fusion
  101.6 0.3 collective-permute-start.18
  101.9 3.1 %collective-permute-start.19 = (bf16[2,256,128]{2,1,0:T(8,128)(2,1)S(1)}, bf16[2,256,128]{2,1,0:T(8,128)(2,1)S(1)}, u32[]{:S(2)}, u32[]{:S(2)}) collective-permute-start(bf16[2,256,128]{2,1,0:T(8,128)(2,1)S(1)} %get-tuple-element.77), channel_id=1, source_target_pairs={{0,96},{8,168},{32,128},{40,200},{64,160},{72,232},{96,192},{104,8... | collective-permute-start | bytes 393224 | tf_op jit(solution)/shard_map/ppermute | solution.py:389
  105.0 4.9 %all-to-all-done.4.parts = bf16[32,32,128]{2,1,0:T(8,128)(2,1)S(1)} async-done(((bf16[32,32,128]{2,1,0:T(8,128)(2,1)}), bf16[32,32,128]{2,1,0:T(8,128)(2,1)S(1)}, u32[]{:S(2)}, u32[]{:S(2)}) %all-to-all-start.4) | async-done | bytes 262176 | tf_op jit(solution)/shard_map/all_to_all | solution.py:422
  109.9 0.7 grad.1
  110.6 0.0 collective-permute-done.11
  110.6 0.1 add_add_fusion.1
  110.7 1.9 %collective-permute-start.15 = (bf16[2,256,128]{2,1,0:T(8,128)(2,1)S(1)}, bf16[2,256,128]{2,1,0:T(8,128)(2,1)S(1)}, u32[]{:S(2)}, u32[]{:S(2)}) collective-permute-start(bf16[2,256,128]{2,1,0:T(8,128)(2,1)S(1)} %slice.20), channel_id=1, source_target_pairs={{0,32},{8,232},{32,64},{40,8},{64,96},{72,40},{96,128},{104,72},{1... | collective-permute-start | bytes 393224 | tf_op jit(solution)/shard_map/ppermute | solution.py:389
  112.6 2.1 %collective-permute-start.20 = (bf16[1,256,128]{2,1,0:T(8,128)(2,1)S(1)}, bf16[1,256,128]{2,1,0:T(8,128)(2,1)S(1)}, u32[]{:S(2)}, u32[]{:S(2)}) collective-permute-start(bf16[1,256,128]{2,1,0:T(8,128)(2,1)S(1)} %get-tuple-element.76), channel_id=1, source_target_pairs={{0,128},{8,136},{32,160},{40,168},{64,192},{72,200},{96,224},{104,... | collective-permute-start | bytes 196616 | tf_op jit(solution)/shard_map/ppermute | solution.py:389
  114.6 3.4 %all-to-all-start.5 = ((f32[8,32,128]{2,1,0:T(8,128)}), f32[8,32,128]{2,1,0:T(8,128)S(1)}, u32[]{:S(2)}, u32[]{:S(2)}) async-start(f32[8,32,128]{2,1,0:T(8,128)} %grad.1), calls=%async_computation.5 | async-start | bytes 262144 | tf_op jit(solution)/shard_map/all_to_all | solution.py:427
  118.0 0.0 collective-permute-done.19.three
  118.0 3.4 %collective-permute-done.20.four = bf16[1,256,128]{2,1,0:T(8,128)(2,1)S(1)} collective-permute-done((bf16[1,256,128]{2,1,0:T(8,128)(2,1)S(1)}, bf16[1,256,128]{2,1,0:T(8,128)(2,1)S(1)}, u32[]{:S(2)}, u32[]{:S(2)}) %collective-permute-start.20) | collective-permute-done | bytes 65568 | tf_op jit(solution)/shard_map/ppermute | solution.py:389
  121.5 0.0 collective-permute-done.15.one
  121.5 0.1 fold.1
  121.5 0.1 collective-permute-start.21
  121.6 4.4 %all-to-all-done.5.pieces = f32[8,32,128]{2,1,0:T(8,128)S(1)} async-done(((f32[8,32,128]{2,1,0:T(8,128)}), f32[8,32,128]{2,1,0:T(8,128)S(1)}, u32[]{:S(2)}, u32[]{:S(2)}) %all-to-all-start.5) | async-done | bytes 131104 | tf_op jit(solution)/shard_map/all_to_all | solution.py:427
  126.0 0.0 collective-permute-done.21.got
  126.0 0.7 final.1
  (17 shorter events, 0.1 us)
Async XLA Ops:
  0.6 10.0 %copy-start.1 = (bf16[256,128]{1,0:T(8,128)(2,1)S(1)}, bf16[256,128]{1,0:T(8,128)(2,1)}, u32[]{:S(2)}) copy-start(bf16[256,128]{1,0:T(8,128)(2,1)} %features.1) | copy-start | bytes 196612
  0.6 8.5 %collective-permute-start = (bf16[256,128]{1,0:T(8,128)(2,1)}, bf16[256,128]{1,0:T(8,128)(2,1)S(1)}, u32[]{:S(2)}, u32[]{:S(2)}) collective-permute-start(bf16[256,128]{1,0:T(8,128)(2,1)} %features.1), channel_id=1, source_target_pairs={{0,16},{16,0},{1,17},{17,1},{2,18},{18,2},{3,19},{19,3},{4,20},{20... | collective-permute-start | bytes 196616 | tf_op jit(solution)/shard_map/ppermute | solution.py:392
  3.0 6.7 %collective-permute-start.1 = (bf16[256,128]{1,0:T(8,128)(2,1)}, bf16[256,128]{1,0:T(8,128)(2,1)S(1)}, u32[]{:S(2)}, u32[]{:S(2)}) collective-permute-start(bf16[256,128]{1,0:T(8,128)(2,1)} %features.1), channel_id=1, source_target_pairs={{0,8},{8,0},{1,9},{9,1},{2,10},{10,2},{3,11},{11,3},{4,12},{12,4},... | collective-permute-start | bytes 196616 | tf_op jit(solution)/shard_map/ppermute | solution.py:392
  3.8 45.8 %copy-start = (bf16[256,128,128]{2,1,0:T(8,128)(2,1)S(1)}, bf16[256,128,128]{2,1,0:T(8,128)(2,1)}, u32[]{:S(2)}) copy-start(bf16[256,128,128]{2,1,0:T(8,128)(2,1)} %tiles.9) | copy-start | bytes 25165828
  9.1 1.5 %collective-permute-start.2 = (bf16[256,128]{1,0:T(8,128)(2,1)S(1)}, bf16[256,128]{1,0:T(8,128)(2,1)S(1)}, u32[]{:S(2)}, u32[]{:S(2)}) collective-permute-start(bf16[256,128]{1,0:T(8,128)(2,1)S(1)} %collective-permute-done.two), channel_id=1, source_target_pairs={{0,8},{8,0},{1,9},{9,1},{2,10},{10,2},{3,11},{11,3},{4,12},{12,4},... | collective-permute-start | bytes 196616 | tf_op jit(solution)/shard_map/ppermute | solution.py:392
  10.7 37.7 %collective-permute-start.3 = (bf16[4,256,128]{2,1,0:T(8,128)(2,1)S(1)}, bf16[4,256,128]{2,1,0:T(8,128)(2,1)S(1)}, u32[]{:S(2)}, u32[]{:S(2)}) collective-permute-start(bf16[4,256,128]{2,1,0:T(8,128)(2,1)S(1)} %get-tuple-element.45.refs_0_), channel_id=1, source_target_pairs={{0,32},{8,232},{32,64},{40,8},{64,96},{72,40},{96,128},{104,72},{1... | collective-permute-start | bytes 786440 | tf_op jit(solution)/shard_map/ppermute | solution.py:389
  10.9 37.6 %collective-permute-start.4 = (bf16[4,256,128]{2,1,0:T(8,128)(2,1)S(1)}, bf16[4,256,128]{2,1,0:T(8,128)(2,1)S(1)}, u32[]{:S(2)}, u32[]{:S(2)}) collective-permute-start(bf16[4,256,128]{2,1,0:T(8,128)(2,1)S(1)} %get-tuple-element.45.refs_0_), channel_id=1, source_target_pairs={{0,64},{8,200},{32,96},{40,232},{64,128},{72,8},{96,160},{104,40},... | collective-permute-start | bytes 786440 | tf_op jit(solution)/shard_map/ppermute | solution.py:389
  14.1 34.3 %collective-permute-start.5 = (bf16[4,256,128]{2,1,0:T(8,128)(2,1)S(1)}, bf16[4,256,128]{2,1,0:T(8,128)(2,1)S(1)}, u32[]{:S(2)}, u32[]{:S(2)}) collective-permute-start(bf16[4,256,128]{2,1,0:T(8,128)(2,1)S(1)} %get-tuple-element.45.refs_0_), channel_id=1, source_target_pairs={{0,96},{8,168},{32,128},{40,200},{64,160},{72,232},{96,192},{104,8... | collective-permute-start | bytes 786440 | tf_op jit(solution)/shard_map/ppermute | solution.py:389
  18.2 30.2 %collective-permute-start.6 = (bf16[2,256,128]{2,1,0:T(8,128)(2,1)S(1)}, bf16[2,256,128]{2,1,0:T(8,128)(2,1)S(1)}, u32[]{:S(2)}, u32[]{:S(2)}) collective-permute-start(bf16[2,256,128]{2,1,0:T(8,128)(2,1)S(1)} %get-tuple-element.46), channel_id=1, source_target_pairs={{0,128},{8,136},{32,160},{40,168},{64,192},{72,200},{96,224},{104,... | collective-permute-start | bytes 393224 | tf_op jit(solution)/shard_map/ppermute | solution.py:389
  48.4 4.0 %collective-permute-start.7 = (bf16[4,256,128]{2,1,0:T(8,128)(2,1)S(1)}, bf16[4,256,128]{2,1,0:T(8,128)(2,1)S(1)}, u32[]{:S(2)}, u32[]{:S(2)}) collective-permute-start(bf16[4,256,128]{2,1,0:T(8,128)(2,1)S(1)} %collective-permute-done.3.refs_1_), channel_id=1, source_target_pairs={{0,8},{8,0},{1,9},{9,1},{2,10},{10,2},{3,11},{11,3},{4,12},{12,4},... | collective-permute-start | bytes 786440 | tf_op jit(solution)/shard_map/ppermute | solution.py:392
  48.5 3.9 %collective-permute-start.8 = (bf16[4,256,128]{2,1,0:T(8,128)(2,1)S(1)}, bf16[4,256,128]{2,1,0:T(8,128)(2,1)S(1)}, u32[]{:S(2)}, u32[]{:S(2)}) collective-permute-start(bf16[4,256,128]{2,1,0:T(8,128)(2,1)S(1)} %collective-permute-done.4.refs_2_), channel_id=1, source_target_pairs={{0,8},{8,0},{1,9},{9,1},{2,10},{10,2},{3,11},{11,3},{4,12},{12,4},... | collective-permute-start | bytes 786440 | tf_op jit(solution)/shard_map/ppermute | solution.py:392
  49.0 3.4 %collective-permute-start.9 = (bf16[4,256,128]{2,1,0:T(8,128)(2,1)S(1)}, bf16[4,256,128]{2,1,0:T(8,128)(2,1)S(1)}, u32[]{:S(2)}, u32[]{:S(2)}) collective-permute-start(bf16[4,256,128]{2,1,0:T(8,128)(2,1)S(1)} %collective-permute-done.5.refs_3_), channel_id=1, source_target_pairs={{0,8},{8,0},{1,9},{9,1},{2,10},{10,2},{3,11},{11,3},{4,12},{12,4},... | collective-permute-start | bytes 786440 | tf_op jit(solution)/shard_map/ppermute | solution.py:392
  49.1 3.3 %collective-permute-start.10 = (bf16[2,256,128]{2,1,0:T(8,128)(2,1)S(1)}, bf16[2,256,128]{2,1,0:T(8,128)(2,1)S(1)}, u32[]{:S(2)}, u32[]{:S(2)}) collective-permute-start(bf16[2,256,128]{2,1,0:T(8,128)(2,1)S(1)} %collective-permute-done.6.refs_4_), channel_id=1, source_target_pairs={{0,8},{8,0},{1,9},{9,1},{2,10},{10,2},{3,11},{11,3},{4,12},{12,4},... | collective-permute-start | bytes 393224 | tf_op jit(solution)/shard_map/ppermute | solution.py:392
  52.4 17.0 %copy-start.2 = (bf16[256,256]{1,0:T(8,128)(2,1)S(1)}, bf16[256,256]{1,0:T(8,128)(2,1)}, u32[]{:S(2)}) copy-start(bf16[256,256]{1,0:T(8,128)(2,1)} %cotangent.1) | copy-start | bytes 393220
  52.4 17.0 %copy-start.3 = (bf16[128,256]{1,0:T(8,128)(2,1)S(1)}, bf16[128,256]{1,0:T(8,128)(2,1)}, u32[]{:S(2)}) copy-start(bf16[128,256]{1,0:T(8,128)(2,1)} %weight.1) | copy-start | bytes 196612
  52.4 17.0 %copy-start.4 = (f32[256]{0:T(256)S(1)}, f32[256]{0:T(256)}, u32[]{:S(2)}) copy-start(f32[256]{0:T(256)} %param.14) | copy-start | bytes 3076
  88.0 3.9 %collective-permute-start.13 = (bf16[4,256,128]{2,1,0:T(8,128)(2,1)S(1)}, bf16[4,256,128]{2,1,0:T(8,128)(2,1)S(1)}, u32[]{:S(2)}, u32[]{:S(2)}) collective-permute-start(bf16[4,256,128]{2,1,0:T(8,128)(2,1)S(1)} %get-tuple-element.61), channel_id=1, source_target_pairs={{0,8},{8,0},{1,9},{9,1},{2,10},{10,2},{3,11},{11,3},{4,12},{12,4},... | collective-permute-start | bytes 786440 | tf_op jit(solution)/shard_map/ppermute | solution.py:392
  88.1 3.8 %collective-permute-start.12 = (bf16[4,256,128]{2,1,0:T(8,128)(2,1)S(1)}, bf16[4,256,128]{2,1,0:T(8,128)(2,1)S(1)}, u32[]{:S(2)}, u32[]{:S(2)}) collective-permute-start(bf16[4,256,128]{2,1,0:T(8,128)(2,1)S(1)} %get-tuple-element.59), channel_id=1, source_target_pairs={{0,8},{8,0},{1,9},{9,1},{2,10},{10,2},{3,11},{11,3},{4,12},{12,4},... | collective-permute-start | bytes 786440 | tf_op jit(solution)/shard_map/ppermute | solution.py:392
  88.6 9.7 %collective-permute-start.16 = (bf16[4,256,128]{2,1,0:T(8,128)(2,1)S(1)}, bf16[4,256,128]{2,1,0:T(8,128)(2,1)S(1)}, u32[]{:S(2)}, u32[]{:S(2)}) collective-permute-start(bf16[4,256,128]{2,1,0:T(8,128)(2,1)S(1)} %get-tuple-element.67), channel_id=1, source_target_pairs={{0,8},{8,0},{1,9},{9,1},{2,10},{10,2},{3,11},{11,3},{4,12},{12,4},... | collective-permute-start | bytes 786440 | tf_op jit(solution)/shard_map/ppermute | solution.py:392
  92.1 9.4 %collective-permute-start.17 = (bf16[4,256,128]{2,1,0:T(8,128)(2,1)S(1)}, bf16[4,256,128]{2,1,0:T(8,128)(2,1)S(1)}, u32[]{:S(2)}, u32[]{:S(2)}) collective-permute-start(bf16[4,256,128]{2,1,0:T(8,128)(2,1)S(1)} %add.19), channel_id=1, source_target_pairs={{0,16},{16,0},{1,17},{17,1},{2,18},{18,2},{3,19},{19,3},{4,20},{20... | collective-permute-start | bytes 786440 | tf_op jit(solution)/shard_map/ppermute | solution.py:392
  93.2 16.7 %all-to-all-start.4 = ((bf16[32,32,128]{2,1,0:T(8,128)(2,1)}), bf16[32,32,128]{2,1,0:T(8,128)(2,1)S(1)}, u32[]{:S(2)}, u32[]{:S(2)}) async-start(bf16[32,32,128]{2,1,0:T(8,128)(2,1)} %get-tuple-element.64), calls=%async_computation.4 | async-start | bytes 524288 | tf_op jit(solution)/shard_map/all_to_all | solution.py:422
  97.7 12.9 %collective-permute-start.11 = (bf16[4,256,128]{2,1,0:T(8,128)(2,1)S(1)}, bf16[4,256,128]{2,1,0:T(8,128)(2,1)S(1)}, u32[]{:S(2)}, u32[]{:S(2)}) collective-permute-start(bf16[4,256,128]{2,1,0:T(8,128)(2,1)S(1)} %get-tuple-element.57), channel_id=1, source_target_pairs={{0,8},{8,0},{1,9},{9,1},{2,10},{10,2},{3,11},{11,3},{4,12},{12,4},... | collective-permute-start | bytes 786440 | tf_op jit(solution)/shard_map/ppermute | solution.py:392
  97.9 12.6 %collective-permute-start.14 = (bf16[4,256,128]{2,1,0:T(8,128)(2,1)S(1)}, bf16[4,256,128]{2,1,0:T(8,128)(2,1)S(1)}, u32[]{:S(2)}, u32[]{:S(2)}) collective-permute-start(bf16[4,256,128]{2,1,0:T(8,128)(2,1)S(1)} %add.20), channel_id=1, source_target_pairs={{0,16},{16,0},{1,17},{17,1},{2,18},{18,2},{3,19},{19,3},{4,20},{20... | collective-permute-start | bytes 786440 | tf_op jit(solution)/shard_map/ppermute | solution.py:392
  101.6 16.4 %collective-permute-start.18 = (bf16[2,256,128]{2,1,0:T(8,128)(2,1)S(1)}, bf16[2,256,128]{2,1,0:T(8,128)(2,1)S(1)}, u32[]{:S(2)}, u32[]{:S(2)}) collective-permute-start(bf16[2,256,128]{2,1,0:T(8,128)(2,1)S(1)} %get-tuple-element.78), channel_id=1, source_target_pairs={{0,64},{8,200},{32,96},{40,232},{64,128},{72,8},{96,160},{104,40},... | collective-permute-start | bytes 393224 | tf_op jit(solution)/shard_map/ppermute | solution.py:389
  101.9 16.1 %collective-permute-start.19 = (bf16[2,256,128]{2,1,0:T(8,128)(2,1)S(1)}, bf16[2,256,128]{2,1,0:T(8,128)(2,1)S(1)}, u32[]{:S(2)}, u32[]{:S(2)}) collective-permute-start(bf16[2,256,128]{2,1,0:T(8,128)(2,1)S(1)} %get-tuple-element.77), channel_id=1, source_target_pairs={{0,96},{8,168},{32,128},{40,200},{64,160},{72,232},{96,192},{104,8... | collective-permute-start | bytes 393224 | tf_op jit(solution)/shard_map/ppermute | solution.py:389
  110.7 10.8 %collective-permute-start.15 = (bf16[2,256,128]{2,1,0:T(8,128)(2,1)S(1)}, bf16[2,256,128]{2,1,0:T(8,128)(2,1)S(1)}, u32[]{:S(2)}, u32[]{:S(2)}) collective-permute-start(bf16[2,256,128]{2,1,0:T(8,128)(2,1)S(1)} %slice.20), channel_id=1, source_target_pairs={{0,32},{8,232},{32,64},{40,8},{64,96},{72,40},{96,128},{104,72},{1... | collective-permute-start | bytes 393224 | tf_op jit(solution)/shard_map/ppermute | solution.py:389
  112.6 8.9 %collective-permute-start.20 = (bf16[1,256,128]{2,1,0:T(8,128)(2,1)S(1)}, bf16[1,256,128]{2,1,0:T(8,128)(2,1)S(1)}, u32[]{:S(2)}, u32[]{:S(2)}) collective-permute-start(bf16[1,256,128]{2,1,0:T(8,128)(2,1)S(1)} %get-tuple-element.76), channel_id=1, source_target_pairs={{0,128},{8,136},{32,160},{40,168},{64,192},{72,200},{96,224},{104,... | collective-permute-start | bytes 196616 | tf_op jit(solution)/shard_map/ppermute | solution.py:389
  114.6 11.4 %all-to-all-start.5 = ((f32[8,32,128]{2,1,0:T(8,128)}), f32[8,32,128]{2,1,0:T(8,128)S(1)}, u32[]{:S(2)}, u32[]{:S(2)}) async-start(f32[8,32,128]{2,1,0:T(8,128)} %grad.1), calls=%async_computation.5 | async-start | bytes 262144 | tf_op jit(solution)/shard_map/all_to_all | solution.py:427
  121.5 4.5 %collective-permute-start.21 = (bf16[256,128]{1,0:T(8,128)(2,1)S(1)}, bf16[256,128]{1,0:T(8,128)(2,1)S(1)}, u32[]{:S(2)}, u32[]{:S(2)}) collective-permute-start(bf16[256,128]{1,0:T(8,128)(2,1)S(1)} %get-tuple-element.70), channel_id=1, source_target_pairs={{0,8},{8,0},{1,9},{9,1},{2,10},{10,2},{3,11},{11,3},{4,12},{12,4},... | collective-permute-start | bytes 196616 | tf_op jit(solution)/shard_map/ppermute | solution.py:392

commit v4 on v3

--- a/solution.py
+++ b/solution.py
@@ -257,8 +257,8 @@
     )(parts, features, scale_col, scale_row, weight, bias, cotangent)
 
 
-LONG = ((3, 0), (3, 1), (2, 0), (2, 1))
-SHORT = ((1, 0), (1, 1), (4, 0), (0, 0))
+LONG = ((3, 0), (3, 1), (2, 0), (2, 1), (4, 0))
+SHORT = ((1, 0), (1, 1), (0, 0))
 
 
 def backward_kernel(length, mine, meta, tiles, back, *outs):
@@ -292,7 +292,10 @@
 def backward_call(length, mine, meta, tiles, back):
     height, width = back.shape[1:]
     blocks = tiles.shape[0] // SLOTS
-    shapes = [jax.ShapeDtypeStruct((len(LONG), 2 * TILE, width), BF16)] * 4
+    shapes = [
+        jax.ShapeDtypeStruct((len(group), 2 * TILE, width), BF16)
+        for group in (LONG, SHORT, LONG, SHORT)
+    ]
     if mine:
         shapes.append(jax.ShapeDtypeStruct((blocks, height - 2 * TILE, width), BF16))
     return pl.pallas_call(
@@ -422,12 +425,12 @@
     piece = lax.all_to_all(piece, ("zed", "pair", "core"), 0, 0, tiled=True)
     piece = grad_call(piece, replicas)
     reach = sums[2] + other[0]
-    three, two = along(reach[:2], 3), along(reach[2:], 2)
+    three, two, four = along(reach[:2], 3), along(reach[2:4], 2), along(reach[4:], 4)
     other[1], piece = lax.optimization_barrier((other[1], piece))
     piece = lax.all_to_all(piece, "rep", 0, 0, tiled=True)
     close = sums[3] + other[1]
-    one, four = along(close[:2], 1), along(close[2:3], 4)
-    keep, give = fold_call((one, two, three, four), close[3:])
+    one = along(close[:2], 1)
+    keep, give = fold_call((one, two, three, four), close[2:])
     grad_features, grad_weight = final_call(
         keep, swap(give, "core"), back_own, scale_row, piece
     )

time: 127 us -> 127 us (level); the launches traced: 127 us -> 125 us
  starting transfers between devices: 29.9 us -> 26.3 us
  waiting for transfers between devices: 16.9 us -> 19.3 us
    ppermute x8, starting transfers between devices: 15.5 us -> 11.9 us  [along(): return lax.ppermute(value, ('zed', 'core'), moves)]
    ppermute x14, waiting for transfers between devices: 4.12 us -> 6.52 us  [swap(): return lax.ppermute(value, axis, SWAP)]
where the time goes in v4:
time: 127 us; the launch traced here: 125 us
  blocking collectives  59.1 us (47%)
  starting transfers between devices  26.3 us (21%)
  waiting for transfers between devices  19.3 us (15%)
  Pallas kernels  18.9 us (15%)
    all_to_all x1, blocking collectives, body(): scales = lax.all_to_all(spread, ('zed', 'pair', 'core'), 0, 0, tiled=True)  15.7 us
    all_to_all x1, blocking collectives, body(): back = lax.all_to_all(pay, 'rep', 0, 0, tiled=True)  15.2 us
    all_to_all x1, blocking collectives, body(): lax.all_to_all(sums.reshape(replicas, sub, width), 'rep', 0, 0, tiled=True)  14.4 us
    all_to_all x1, blocking collectives, body(): lax.all_to_all(partial.reshape(replicas, sub // TILE, TILE), 'rep', 0, 0,...  13.8 us
    ppermute x8, starting transfers between devices, along(): return lax.ppermute(value, ('zed', 'core'), moves)  11.9 us
    ppermute x14, waiting for transfers between devices, swap(): return lax.ppermute(value, axis, SWAP)  6.52 us
    ppermute x14, starting transfers between devices, swap(): return lax.ppermute(value, axis, SWAP)  6.15 us
    pallas_call x2, Pallas kernels, backward_call(): pl.pallas_call(functools.partial(backward_kernel, length, mine), in_specs...  5.59 us
  transfers between devices with their start and end apart: 24, of which 5 were waited for; matrix products, arithmetic and copies ran while one was open for 1% of the time, Pallas kernels for 10%

profile of v4, /device:TPU:2, one launch (start us, length us, event | category | flops | bytes accessed | tf_op | source)
XLA Modules:
  0.0 125.5 jit_solution(10650158474635687323)
XLA Ops:
  0.6 2.4 %collective-permute-start = (bf16[256,128]{1,0:T(8,128)(2,1)}, bf16[256,128]{1,0:T(8,128)(2,1)S(1)}, u32[]{:S(2)}, u32[]{:S(2)}) collective-permute-start(bf16[256,128]{1,0:T(8,128)(2,1)} %features.1), channel_id=1, source_target_pairs={{0,16},{16,0},{1,17},{17,1},{2,18},{18,2},{3,19},{19,3},{4,20},{20... | collective-permute-start | bytes 196616 | tf_op jit(solution)/shard_map/ppermute | solution.py:395
  3.0 0.0 collective-permute-start.1
  3.0 0.8 concatenate.3.meta
  3.8 5.3 %degree.1 = f32[16,128]{1,0:T(8,128)S(1)} custom-call(s32[1,547]{1,0:T(1,128)S(1)} %concatenate.3.meta, bf16[256,128,128]{2,1,0:T(8,128)(2,1)} %tiles.9), custom_call_target="tpu_custom_call" | custom-call | tf_op jit(solution)/shard_map/degree/pallas_call | solution.py:80
  9.1 0.0 collective-permute-done.two
  9.1 0.5 collective-permute-start.2
  9.6 0.0 collective-permute-done.1.three
  9.6 0.9 collective-permute-done.2.four
  10.6 0.3 collective-permute-start.3
  10.9 3.2 %collective-permute-start.4 = (bf16[4,256,128]{2,1,0:T(8,128)(2,1)S(1)}, bf16[4,256,128]{2,1,0:T(8,128)(2,1)S(1)}, u32[]{:S(2)}, u32[]{:S(2)}) collective-permute-start(bf16[4,256,128]{2,1,0:T(8,128)(2,1)S(1)} %get-tuple-element.45.refs_0_), channel_id=1, source_target_pairs={{0,64},{8,200},{32,96},{40,232},{64,128},{72,8},{96,160},{104,40},... | collective-permute-start | bytes 786440 | tf_op jit(solution)/shard_map/ppermute | solution.py:392
  14.1 4.1 %collective-permute-start.5 = (bf16[4,256,128]{2,1,0:T(8,128)(2,1)S(1)}, bf16[4,256,128]{2,1,0:T(8,128)(2,1)S(1)}, u32[]{:S(2)}, u32[]{:S(2)}) collective-permute-start(bf16[4,256,128]{2,1,0:T(8,128)(2,1)S(1)} %get-tuple-element.45.refs_0_), channel_id=1, source_target_pairs={{0,96},{8,168},{32,128},{40,200},{64,160},{72,232},{96,192},{104,8... | collective-permute-start | bytes 786440 | tf_op jit(solution)/shard_map/ppermute | solution.py:392
  18.2 0.5 collective-permute-start.6
  18.7 13.8 %all_to_all.30.parts = f32[8,2,128]{2,1,0:T(2,128)S(1)} all-to-all(f32[8,2,128]{2,1,0:T(2,128)S(1)} %bitcast.7), channel_id=1, replica_groups=mesh['zed'=8,'pair'=2,'core'=2,'rep'=8] {'rep'}, dimensions={0} | all-to-all | bytes 16384 | tf_op jit(solution)/shard_map/all_to_all | solution.py:404
  32.5 0.1 scale.1
  32.7 15.7 %all_to_all.31.scales = f32[32,2,128]{2,1,0:T(2,128)S(1)} all-to-all(f32[32,2,128]{2,1,0:T(2,128)S(1)} %get-tuple-element.44), channel_id=1, replica_groups=mesh['zed'=8,'pair'=2,'core'=2,'rep'=8] {'zed','pair','core'}, dimensions={0} | all-to-all | bytes 65536 | tf_op jit(solution)/shard_map/all_to_all | solution.py:408
  48.4 0.0 collective-permute-done.6.refs_4_
  48.4 0.0 collective-permute-done.3.refs_1_
  48.4 0.0 collective-permute-done.4.refs_2_
  48.4 0.0 collective-permute-done.5.refs_3_
  48.4 0.1 collective-permute-start.7
  48.5 0.5 collective-permute-start.8
  49.0 0.1 collective-permute-start.9
  49.1 0.4 collective-permute-start.10
  49.5 2.8 %forward_near.1.refs_0_ = f32[17,128,128]{2,1,0:T(8,128)S(1)} custom-call(s32[1,547]{1,0:T(1,128)S(1)} %concatenate.3.meta, bf16[256,128,128]{2,1,0:T(8,128)(2,1)S(1)} %copy-done, f32[32,2,128]{2,1,0:T(2,128)S(1)} %all_to_all.31.scales, bf16[4,256,128]{2,1,0:T(8,128)(2,1)S(1)} %get-tuple-element.45.refs_0_, ...), custom_call_target="tpu_custom_call" | custom-call | tf_op jit(solution)/shard_map/forward_near/pallas_call | solution.py:196
  52.4 0.0 copy-start.2
  52.4 0.0 copy-start.3
  52.4 0.0 copy-start.4
  52.4 0.0 collective-permute-done.10.refs_4_
  52.4 0.0 collective-permute-done.7.refs_1_
  52.4 0.0 collective-permute-done.8.refs_2_
  52.4 2.5 %forward_far.1 = bf16[16,128,128]{2,1,0:T(8,128)(2,1)S(1)} custom-call(s32[1,547]{1,0:T(1,128)S(1)} %concatenate.3.meta, bf16[256,128,128]{2,1,0:T(8,128)(2,1)S(1)} %copy-done, f32[32,2,128]{2,1,0:T(2,128)S(1)} %all_to_all.31.scales, f32[17,128,128]{2,1,0:T(8,128)S(1)} %forward_near.1.refs_0_, bf16[4,256,128]{2,1,0:T(8,128)(2,1)S(1)} %collective-permute-done.7.refs_1_, ...), custom_call_target="tpu_custom_call" | custom-call | tf_op jit(solution)/shard_map/forward_far/pallas_call | solution.py:196
  54.9 14.4 %all_to_all.32.parts = bf16[8,256,128]{2,1,0:T(8,128)(2,1)S(1)} all-to-all(bf16[8,256,128]{2,1,0:T(8,128)(2,1)S(1)} %bitcast.6), channel_id=1, replica_groups=mesh['zed'=8,'pair'=2,'core'=2,'rep'=8] {'rep'}, dimensions={0} | all-to-all | bytes 1048576 | tf_op jit(solution)/shard_map/all_to_all | solution.py:413
  69.3 1.1 dense.1
  70.4 15.2 %all_to_all.33.back = bf16[8,288,128]{2,1,0:T(8,128)(2,1)S(1)} all-to-all(bf16[8,288,128]{2,1,0:T(8,128)(2,1)S(1)} %get-tuple-element.55), channel_id=1, replica_groups=mesh['zed'=8,'pair'=2,'core'=2,'rep'=8] {'rep'}, dimensions={0} | all-to-all | bytes 1179648 | tf_op jit(solution)/shard_map/all_to_all | solution.py:417
  85.6 2.4 %backward_far.1 = (bf16[5,256,128]{2,1,0:T(8,128)(2,1)S(1)}, bf16[3,256,128]{2,1,0:T(8,128)(2,1)S(1)}, bf16[5,256,128]{2,1,0:T(8,128)(2,1)S(1)}, bf16[3,256,128]{2,1,0:T(8,128)(2,1)S(1)}) custom-call(s32[1,547]{1,0:T(1,128)S(1)} %concatenate.3.meta, bf16[256,128,128]{2,1,0:T(8,128)(2,1)S(1)} %copy-done, bf16[8,288,128]{2,1,0:T(8,128)(2,1)S(1)} %all_to_all.33.back), custom_call_target="tpu_custom_call" | custom-call | tf_op jit(solution)/shard_map/backward_far/pallas_call | solution.py:301
  88.0 0.1 collective-permute-start.12
  88.1 0.5 collective-permute-start.13
  88.6 0.1 collective-permute-start.16
  88.7 3.2 %backward_near.1 = (bf16[5,256,128]{2,1,0:T(8,128)(2,1)S(1)}, bf16[3,256,128]{2,1,0:T(8,128)(2,1)S(1)}, bf16[5,256,128]{2,1,0:T(8,128)(2,1)S(1)}, bf16[3,256,128]{2,1,0:T(8,128)(2,1)S(1)}, bf16[32,32,128]{2,1,0:T(8,128)(2,1)}) custom-call(s32[1,547]{1,0:T(1,128)S(1)} %concatenate.3.meta, bf16[256,128,128]{2,1,0:T(8,128)(2,1)S(1)} %copy-done, ...), custom_call_target="tpu_custom_call" | custom-call | tf_op jit(solution)/shard_map/backward_near/pallas_call | solution.py:301
  91.8 0.0 collective-permute-done.13
  91.9 0.1 add.20
  91.9 0.1 add.19
  92.0 0.8 collective-permute-start.17
  92.8 4.9 %all-to-all-start.4 = ((bf16[32,32,128]{2,1,0:T(8,128)(2,1)}), bf16[32,32,128]{2,1,0:T(8,128)(2,1)S(1)}, u32[]{:S(2)}, u32[]{:S(2)}) async-start(bf16[32,32,128]{2,1,0:T(8,128)(2,1)} %get-tuple-element.64), calls=%async_computation.4 | async-start | bytes 524288 | tf_op jit(solution)/shard_map/all_to_all | solution.py:425
  97.7 0.2 collective-permute-start.11
  97.9 0.4 collective-permute-start.14
  98.3 0.0 collective-permute-done.16
  98.3 5.6 %collective-permute-done.17 = bf16[5,256,128]{2,1,0:T(8,128)(2,1)S(1)} collective-permute-done((bf16[5,256,128]{2,1,0:T(8,128)(2,1)S(1)}, bf16[5,256,128]{2,1,0:T(8,128)(2,1)S(1)}, u32[]{:S(2)}, u32[]{:S(2)}) %collective-permute-start.17) | collective-permute-done | bytes 327712 | tf_op jit(solution)/shard_map/ppermute | solution.py:395
  103.8 0.1 add_add_fusion
  103.9 0.3 collective-permute-start.18
  104.3 0.7 collective-permute-start.19
  104.9 4.9 %all-to-all-done.4.parts = bf16[32,32,128]{2,1,0:T(8,128)(2,1)S(1)} async-done(((bf16[32,32,128]{2,1,0:T(8,128)(2,1)}), bf16[32,32,128]{2,1,0:T(8,128)(2,1)S(1)}, u32[]{:S(2)}, u32[]{:S(2)}) %all-to-all-start.4) | async-done | bytes 262176 | tf_op jit(solution)/shard_map/all_to_all | solution.py:425
  109.8 0.7 grad.1
  110.5 0.0 collective-permute-done.14
  110.5 0.0 collective-permute-done.11
  110.6 1.4 %collective-permute-start.15 = (bf16[2,256,128]{2,1,0:T(8,128)(2,1)S(1)}, bf16[2,256,128]{2,1,0:T(8,128)(2,1)S(1)}, u32[]{:S(2)}, u32[]{:S(2)}) collective-permute-start(bf16[2,256,128]{2,1,0:T(8,128)(2,1)S(1)} %slice.20), channel_id=1, source_target_pairs={{0,32},{8,232},{32,64},{40,8},{64,96},{72,40},{96,128},{104,72},{1... | collective-permute-start | bytes 393224 | tf_op jit(solution)/shard_map/ppermute | solution.py:392
  112.0 1.4 %collective-permute-start.20 = (bf16[1,256,128]{2,1,0:T(8,128)(2,1)S(1)}, bf16[1,256,128]{2,1,0:T(8,128)(2,1)S(1)}, u32[]{:S(2)}, u32[]{:S(2)}) collective-permute-start(bf16[1,256,128]{2,1,0:T(8,128)(2,1)S(1)} %slice.23), channel_id=1, source_target_pairs={{0,128},{8,136},{32,160},{40,168},{64,192},{72,200},{96,224},{104,... | collective-permute-start | bytes 196616 | tf_op jit(solution)/shard_map/ppermute | solution.py:392
  113.3 3.4 %all-to-all-start.5 = ((f32[8,32,128]{2,1,0:T(8,128)}), f32[8,32,128]{2,1,0:T(8,128)S(1)}, u32[]{:S(2)}, u32[]{:S(2)}) async-start(f32[8,32,128]{2,1,0:T(8,128)} %grad.1), calls=%async_computation.5 | async-start | bytes 262144 | tf_op jit(solution)/shard_map/all_to_all | solution.py:430
  116.7 4.3 %collective-permute-done.20.four = bf16[1,256,128]{2,1,0:T(8,128)(2,1)S(1)} collective-permute-done((bf16[1,256,128]{2,1,0:T(8,128)(2,1)S(1)}, bf16[1,256,128]{2,1,0:T(8,128)(2,1)S(1)}, u32[]{:S(2)}, u32[]{:S(2)}) %collective-permute-start.20) | collective-permute-done | bytes 65568 | tf_op jit(solution)/shard_map/ppermute | solution.py:392
  121.1 0.1 fold.1
  121.2 0.1 collective-permute-start.21
  121.3 3.5 %all-to-all-done.5.pieces = f32[8,32,128]{2,1,0:T(8,128)S(1)} async-done(((f32[8,32,128]{2,1,0:T(8,128)}), f32[8,32,128]{2,1,0:T(8,128)S(1)}, u32[]{:S(2)}, u32[]{:S(2)}) %all-to-all-start.5) | async-done | bytes 131104 | tf_op jit(solution)/shard_map/all_to_all | solution.py:430
  124.8 0.0 collective-permute-done.21.got
  124.8 0.7 final.1
  (18 shorter events, 0.2 us)
Async XLA Ops:
  0.6 9.9 %copy-start.1 = (bf16[256,128]{1,0:T(8,128)(2,1)S(1)}, bf16[256,128]{1,0:T(8,128)(2,1)}, u32[]{:S(2)}) copy-start(bf16[256,128]{1,0:T(8,128)(2,1)} %features.1) | copy-start | bytes 196612
  0.6 8.4 %collective-permute-start = (bf16[256,128]{1,0:T(8,128)(2,1)}, bf16[256,128]{1,0:T(8,128)(2,1)S(1)}, u32[]{:S(2)}, u32[]{:S(2)}) collective-permute-start(bf16[256,128]{1,0:T(8,128)(2,1)} %features.1), channel_id=1, source_target_pairs={{0,16},{16,0},{1,17},{17,1},{2,18},{18,2},{3,19},{19,3},{4,20},{20... | collective-permute-start | bytes 196616 | tf_op jit(solution)/shard_map/ppermute | solution.py:395
  3.0 6.6 %collective-permute-start.1 = (bf16[256,128]{1,0:T(8,128)(2,1)}, bf16[256,128]{1,0:T(8,128)(2,1)S(1)}, u32[]{:S(2)}, u32[]{:S(2)}) collective-permute-start(bf16[256,128]{1,0:T(8,128)(2,1)} %features.1), channel_id=1, source_target_pairs={{0,8},{8,0},{1,9},{9,1},{2,10},{10,2},{3,11},{11,3},{4,12},{12,4},... | collective-permute-start | bytes 196616 | tf_op jit(solution)/shard_map/ppermute | solution.py:395
  3.8 45.7 %copy-start = (bf16[256,128,128]{2,1,0:T(8,128)(2,1)S(1)}, bf16[256,128,128]{2,1,0:T(8,128)(2,1)}, u32[]{:S(2)}) copy-start(bf16[256,128,128]{2,1,0:T(8,128)(2,1)} %tiles.9) | copy-start | bytes 25165828
  9.1 1.4 %collective-permute-start.2 = (bf16[256,128]{1,0:T(8,128)(2,1)S(1)}, bf16[256,128]{1,0:T(8,128)(2,1)S(1)}, u32[]{:S(2)}, u32[]{:S(2)}) collective-permute-start(bf16[256,128]{1,0:T(8,128)(2,1)S(1)} %collective-permute-done.two), channel_id=1, source_target_pairs={{0,8},{8,0},{1,9},{9,1},{2,10},{10,2},{3,11},{11,3},{4,12},{12,4},... | collective-permute-start | bytes 196616 | tf_op jit(solution)/shard_map/ppermute | solution.py:395
  10.6 37.8 %collective-permute-start.3 = (bf16[4,256,128]{2,1,0:T(8,128)(2,1)S(1)}, bf16[4,256,128]{2,1,0:T(8,128)(2,1)S(1)}, u32[]{:S(2)}, u32[]{:S(2)}) collective-permute-start(bf16[4,256,128]{2,1,0:T(8,128)(2,1)S(1)} %get-tuple-element.45.refs_0_), channel_id=1, source_target_pairs={{0,32},{8,232},{32,64},{40,8},{64,96},{72,40},{96,128},{104,72},{1... | collective-permute-start | bytes 786440 | tf_op jit(solution)/shard_map/ppermute | solution.py:392
  10.9 37.5 %collective-permute-start.4 = (bf16[4,256,128]{2,1,0:T(8,128)(2,1)S(1)}, bf16[4,256,128]{2,1,0:T(8,128)(2,1)S(1)}, u32[]{:S(2)}, u32[]{:S(2)}) collective-permute-start(bf16[4,256,128]{2,1,0:T(8,128)(2,1)S(1)} %get-tuple-element.45.refs_0_), channel_id=1, source_target_pairs={{0,64},{8,200},{32,96},{40,232},{64,128},{72,8},{96,160},{104,40},... | collective-permute-start | bytes 786440 | tf_op jit(solution)/shard_map/ppermute | solution.py:392
  14.1 34.3 %collective-permute-start.5 = (bf16[4,256,128]{2,1,0:T(8,128)(2,1)S(1)}, bf16[4,256,128]{2,1,0:T(8,128)(2,1)S(1)}, u32[]{:S(2)}, u32[]{:S(2)}) collective-permute-start(bf16[4,256,128]{2,1,0:T(8,128)(2,1)S(1)} %get-tuple-element.45.refs_0_), channel_id=1, source_target_pairs={{0,96},{8,168},{32,128},{40,200},{64,160},{72,232},{96,192},{104,8... | collective-permute-start | bytes 786440 | tf_op jit(solution)/shard_map/ppermute | solution.py:392
  18.2 30.2 %collective-permute-start.6 = (bf16[2,256,128]{2,1,0:T(8,128)(2,1)S(1)}, bf16[2,256,128]{2,1,0:T(8,128)(2,1)S(1)}, u32[]{:S(2)}, u32[]{:S(2)}) collective-permute-start(bf16[2,256,128]{2,1,0:T(8,128)(2,1)S(1)} %get-tuple-element.46), channel_id=1, source_target_pairs={{0,128},{8,136},{32,160},{40,168},{64,192},{72,200},{96,224},{104,... | collective-permute-start | bytes 393224 | tf_op jit(solution)/shard_map/ppermute | solution.py:392
  48.4 4.0 %collective-permute-start.7 = (bf16[4,256,128]{2,1,0:T(8,128)(2,1)S(1)}, bf16[4,256,128]{2,1,0:T(8,128)(2,1)S(1)}, u32[]{:S(2)}, u32[]{:S(2)}) collective-permute-start(bf16[4,256,128]{2,1,0:T(8,128)(2,1)S(1)} %collective-permute-done.3.refs_1_), channel_id=1, source_target_pairs={{0,8},{8,0},{1,9},{9,1},{2,10},{10,2},{3,11},{11,3},{4,12},{12,4},... | collective-permute-start | bytes 786440 | tf_op jit(solution)/shard_map/ppermute | solution.py:395
  48.5 3.9 %collective-permute-start.8 = (bf16[4,256,128]{2,1,0:T(8,128)(2,1)S(1)}, bf16[4,256,128]{2,1,0:T(8,128)(2,1)S(1)}, u32[]{:S(2)}, u32[]{:S(2)}) collective-permute-start(bf16[4,256,128]{2,1,0:T(8,128)(2,1)S(1)} %collective-permute-done.4.refs_2_), channel_id=1, source_target_pairs={{0,8},{8,0},{1,9},{9,1},{2,10},{10,2},{3,11},{11,3},{4,12},{12,4},... | collective-permute-start | bytes 786440 | tf_op jit(solution)/shard_map/ppermute | solution.py:395
  49.0 3.4 %collective-permute-start.9 = (bf16[4,256,128]{2,1,0:T(8,128)(2,1)S(1)}, bf16[4,256,128]{2,1,0:T(8,128)(2,1)S(1)}, u32[]{:S(2)}, u32[]{:S(2)}) collective-permute-start(bf16[4,256,128]{2,1,0:T(8,128)(2,1)S(1)} %collective-permute-done.5.refs_3_), channel_id=1, source_target_pairs={{0,8},{8,0},{1,9},{9,1},{2,10},{10,2},{3,11},{11,3},{4,12},{12,4},... | collective-permute-start | bytes 786440 | tf_op jit(solution)/shard_map/ppermute | solution.py:395
  49.1 3.3 %collective-permute-start.10 = (bf16[2,256,128]{2,1,0:T(8,128)(2,1)S(1)}, bf16[2,256,128]{2,1,0:T(8,128)(2,1)S(1)}, u32[]{:S(2)}, u32[]{:S(2)}) collective-permute-start(bf16[2,256,128]{2,1,0:T(8,128)(2,1)S(1)} %collective-permute-done.6.refs_4_), channel_id=1, source_target_pairs={{0,8},{8,0},{1,9},{9,1},{2,10},{10,2},{3,11},{11,3},{4,12},{12,4},... | collective-permute-start | bytes 393224 | tf_op jit(solution)/shard_map/ppermute | solution.py:395
  52.4 17.0 %copy-start.2 = (bf16[256,256]{1,0:T(8,128)(2,1)S(1)}, bf16[256,256]{1,0:T(8,128)(2,1)}, u32[]{:S(2)}) copy-start(bf16[256,256]{1,0:T(8,128)(2,1)} %cotangent.1) | copy-start | bytes 393220
  52.4 17.0 %copy-start.3 = (bf16[128,256]{1,0:T(8,128)(2,1)S(1)}, bf16[128,256]{1,0:T(8,128)(2,1)}, u32[]{:S(2)}) copy-start(bf16[128,256]{1,0:T(8,128)(2,1)} %weight.1) | copy-start | bytes 196612
  52.4 17.0 %copy-start.4 = (f32[256]{0:T(256)S(1)}, f32[256]{0:T(256)}, u32[]{:S(2)}) copy-start(f32[256]{0:T(256)} %param.14) | copy-start | bytes 3076
  88.0 3.9 %collective-permute-start.12 = (bf16[5,256,128]{2,1,0:T(8,128)(2,1)S(1)}, bf16[5,256,128]{2,1,0:T(8,128)(2,1)S(1)}, u32[]{:S(2)}, u32[]{:S(2)}) collective-permute-start(bf16[5,256,128]{2,1,0:T(8,128)(2,1)S(1)} %get-tuple-element.59), channel_id=1, source_target_pairs={{0,8},{8,0},{1,9},{9,1},{2,10},{10,2},{3,11},{11,3},{4,12},{12,4},... | collective-permute-start | bytes 983048 | tf_op jit(solution)/shard_map/ppermute | solution.py:395
  88.1 3.8 %collective-permute-start.13 = (bf16[3,256,128]{2,1,0:T(8,128)(2,1)S(1)}, bf16[3,256,128]{2,1,0:T(8,128)(2,1)S(1)}, u32[]{:S(2)}, u32[]{:S(2)}) collective-permute-start(bf16[3,256,128]{2,1,0:T(8,128)(2,1)S(1)} %get-tuple-element.61), channel_id=1, source_target_pairs={{0,8},{8,0},{1,9},{9,1},{2,10},{10,2},{3,11},{11,3},{4,12},{12,4},... | collective-permute-start | bytes 589832 | tf_op jit(solution)/shard_map/ppermute | solution.py:395
  88.6 9.7 %collective-permute-start.16 = (bf16[5,256,128]{2,1,0:T(8,128)(2,1)S(1)}, bf16[5,256,128]{2,1,0:T(8,128)(2,1)S(1)}, u32[]{:S(2)}, u32[]{:S(2)}) collective-permute-start(bf16[5,256,128]{2,1,0:T(8,128)(2,1)S(1)} %get-tuple-element.67), channel_id=1, source_target_pairs={{0,8},{8,0},{1,9},{9,1},{2,10},{10,2},{3,11},{11,3},{4,12},{12,4},... | collective-permute-start | bytes 983048 | tf_op jit(solution)/shard_map/ppermute | solution.py:395
  92.0 11.8 %collective-permute-start.17 = (bf16[5,256,128]{2,1,0:T(8,128)(2,1)S(1)}, bf16[5,256,128]{2,1,0:T(8,128)(2,1)S(1)}, u32[]{:S(2)}, u32[]{:S(2)}) collective-permute-start(bf16[5,256,128]{2,1,0:T(8,128)(2,1)S(1)} %add.19), channel_id=1, source_target_pairs={{0,16},{16,0},{1,17},{17,1},{2,18},{18,2},{3,19},{19,3},{4,20},{20... | collective-permute-start | bytes 983048 | tf_op jit(solution)/shard_map/ppermute | solution.py:395
  92.8 17.0 %all-to-all-start.4 = ((bf16[32,32,128]{2,1,0:T(8,128)(2,1)}), bf16[32,32,128]{2,1,0:T(8,128)(2,1)S(1)}, u32[]{:S(2)}, u32[]{:S(2)}) async-start(bf16[32,32,128]{2,1,0:T(8,128)(2,1)} %get-tuple-element.64), calls=%async_computation.4 | async-start | bytes 524288 | tf_op jit(solution)/shard_map/all_to_all | solution.py:425
  97.7 12.9 %collective-permute-start.11 = (bf16[3,256,128]{2,1,0:T(8,128)(2,1)S(1)}, bf16[3,256,128]{2,1,0:T(8,128)(2,1)S(1)}, u32[]{:S(2)}, u32[]{:S(2)}) collective-permute-start(bf16[3,256,128]{2,1,0:T(8,128)(2,1)S(1)} %get-tuple-element.57), channel_id=1, source_target_pairs={{0,8},{8,0},{1,9},{9,1},{2,10},{10,2},{3,11},{11,3},{4,12},{12,4},... | collective-permute-start | bytes 589832 | tf_op jit(solution)/shard_map/ppermute | solution.py:395
  97.9 12.6 %collective-permute-start.14 = (bf16[3,256,128]{2,1,0:T(8,128)(2,1)S(1)}, bf16[3,256,128]{2,1,0:T(8,128)(2,1)S(1)}, u32[]{:S(2)}, u32[]{:S(2)}) collective-permute-start(bf16[3,256,128]{2,1,0:T(8,128)(2,1)S(1)} %add.20), channel_id=1, source_target_pairs={{0,16},{16,0},{1,17},{17,1},{2,18},{18,2},{3,19},{19,3},{4,20},{20... | collective-permute-start | bytes 589832 | tf_op jit(solution)/shard_map/ppermute | solution.py:395
  103.9 17.1 %collective-permute-start.18 = (bf16[2,256,128]{2,1,0:T(8,128)(2,1)S(1)}, bf16[2,256,128]{2,1,0:T(8,128)(2,1)S(1)}, u32[]{:S(2)}, u32[]{:S(2)}) collective-permute-start(bf16[2,256,128]{2,1,0:T(8,128)(2,1)S(1)} %get-tuple-element.76), channel_id=1, source_target_pairs={{0,64},{8,200},{32,96},{40,232},{64,128},{72,8},{96,160},{104,40},... | collective-permute-start | bytes 393224 | tf_op jit(solution)/shard_map/ppermute | solution.py:392
  104.3 16.8 %collective-permute-start.19 = (bf16[2,256,128]{2,1,0:T(8,128)(2,1)S(1)}, bf16[2,256,128]{2,1,0:T(8,128)(2,1)S(1)}, u32[]{:S(2)}, u32[]{:S(2)}) collective-permute-start(bf16[2,256,128]{2,1,0:T(8,128)(2,1)S(1)} %get-tuple-element.75), channel_id=1, source_target_pairs={{0,96},{8,168},{32,128},{40,200},{64,160},{72,232},{96,192},{104,8... | collective-permute-start | bytes 393224 | tf_op jit(solution)/shard_map/ppermute | solution.py:392
  110.6 10.5 %collective-permute-start.15 = (bf16[2,256,128]{2,1,0:T(8,128)(2,1)S(1)}, bf16[2,256,128]{2,1,0:T(8,128)(2,1)S(1)}, u32[]{:S(2)}, u32[]{:S(2)}) collective-permute-start(bf16[2,256,128]{2,1,0:T(8,128)(2,1)S(1)} %slice.20), channel_id=1, source_target_pairs={{0,32},{8,232},{32,64},{40,8},{64,96},{72,40},{96,128},{104,72},{1... | collective-permute-start | bytes 393224 | tf_op jit(solution)/shard_map/ppermute | solution.py:392
  112.0 9.1 %collective-permute-start.20 = (bf16[1,256,128]{2,1,0:T(8,128)(2,1)S(1)}, bf16[1,256,128]{2,1,0:T(8,128)(2,1)S(1)}, u32[]{:S(2)}, u32[]{:S(2)}) collective-permute-start(bf16[1,256,128]{2,1,0:T(8,128)(2,1)S(1)} %slice.23), channel_id=1, source_target_pairs={{0,128},{8,136},{32,160},{40,168},{64,192},{72,200},{96,224},{104,... | collective-permute-start | bytes 196616 | tf_op jit(solution)/shard_map/ppermute | solution.py:392
  113.3 11.4 %all-to-all-start.5 = ((f32[8,32,128]{2,1,0:T(8,128)}), f32[8,32,128]{2,1,0:T(8,128)S(1)}, u32[]{:S(2)}, u32[]{:S(2)}) async-start(f32[8,32,128]{2,1,0:T(8,128)} %grad.1), calls=%async_computation.5 | async-start | bytes 262144 | tf_op jit(solution)/shard_map/all_to_all | solution.py:430
  121.2 3.6 %collective-permute-start.21 = (bf16[256,128]{1,0:T(8,128)(2,1)S(1)}, bf16[256,128]{1,0:T(8,128)(2,1)S(1)}, u32[]{:S(2)}, u32[]{:S(2)}) collective-permute-start(bf16[256,128]{1,0:T(8,128)(2,1)S(1)} %get-tuple-element.70), channel_id=1, source_target_pairs={{0,8},{8,0},{1,9},{9,1},{2,10},{10,2},{3,11},{11,3},{4,12},{12,4},... | collective-permute-start | bytes 196616 | tf_op jit(solution)/shard_map/ppermute | solution.py:395
